TPU v7x, 512 devices: a whole 4x8x8 slice. The times are simulated.
512 devices in a mesh: space: 64 (over y_hi, z, core), bead: 8 (over y_lo, x).
Axes of the slice: x: 4, y: 8 (y_hi: 4, y_lo: 2; y = y_hi * 2 + y_lo), z: 8, core: 2. Of those that a mesh axis runs over, the one named last changes fastest.
Arguments:
- centroids: float32 [3, 16384], P(None, 'space'), may hold values from 0 to 1
- offsets: float32 [3, 32, 16384], P(None, 'bead', 'space'), may hold values from -1 to 1
- velocities: float32 [3, 32, 16384], P(None, 'bead', 'space'), may hold values from -12 to 12
- charges: float32 [16384], P('space'), may hold values from -3 to 3
- polar: float32 [16384], P('space'), may hold values from 0.4 to 1.6
- masses: float32 [16384], P('space'), may hold values from 1 to 16
- groups: int32 [16384], P('space'), may hold values from 0 to 8191, never falling along the last dimension, each value on 1 to 3 neighbouring positions
- tiles: int32 [128, 4], P('space'), may hold values from 0 to 5, as said below
Outputs:
- dipoles: float32 [3, 32, 16384], P(None, 'bead', 'space')
- forces: float32 [3, 32, 16384], P(None, 'bead', 'space')
- new_velocity: float32 [3, 32, 16384], P(None, 'bead', 'space')
- new_offset: float32 [3, 32, 16384], P(None, 'bead', 'space')
Inputs may be any that keep to these rules, and one draw needn't show every extreme that they name: `tiles`: row c lists 4 different blocks, numbered within the concatenation of the slab before block c's slab (periodically), block c's own slab and the slab after, each of 2 blocks of 128 consecutive atoms.
All inputs are finite; a program needn't handle non-finite values.
Results may differ from a plain program's by a relative error of at most 0.0004.
Values sent between devices are 32-bit elements; how exact they have to be, the bound alone decides.
No kernel may reach another device: no remote copies, remote signals or barrier semaphores. Data moves between devices by JAX's collectives and lax.ppermute only.
A program may use at most 64 MiB of HBM per device.

v0:
```python
import jax
import jax.numpy as jnp
from jax import lax
from jax.sharding import PartitionSpec as P

BLOCK = 128
NT = 4
ITERS = 3


slab_width = 9.0
box_side = 24.0
cut_square = 64.0
thole_coef = 0.39
bond_coef = 4.0
time_step = 0.05
target_temp = 8.0
coupling = 0.5


def extended(array, sides, width):
    for axis, dim in sides:
        count, length = (lax.axis_size(axis), array.shape[dim])
        up = [(i, (i + 1) % count) for i in range(count)]
        down = [(j, i) for i, j in up]
        last = lax.slice_in_dim(array, length - width, length, axis=dim)
        first = lax.slice_in_dim(array, 0, width, axis=dim)
        before = lax.ppermute(last, axis, up)
        after = lax.ppermute(first, axis, down)
        array = jnp.concatenate([before, array, after], axis=dim)
    return array


def shifted(array, axis, by):
    count = lax.axis_size(axis)
    return lax.ppermute(array, axis, [(i, (i + by) % count) for i in range(count)])


def geometry(xi, ai, gi, xj, aj, gj, keep, period):
    delta = xi[:, :, :, None] - xj[:, :, None, :]
    delta = delta - period * jnp.floor(delta / period + 0.5)
    square = jnp.sum(delta * delta, axis=0) + 1.0
    damp = thole_coef * square * jnp.sqrt(square) / jnp.sqrt(ai[:, None] * aj[None, :])
    fade = jnp.exp(-damp)
    lam_three = 1.0 - fade
    lam_five = 1.0 - (1.0 + damp) * fade
    taper = jnp.where(square < cut_square, (1.0 - square / cut_square) ** 2, 0.0)
    weight = taper * jnp.where(gi[:, None] == gj[None, :], 0.0, 1.0) * keep[None, :]
    inv_three = weight * lam_three / (square * jnp.sqrt(square))
    inv_five = 3.0 * weight * lam_five / (square * square * jnp.sqrt(square))
    return (delta, inv_three, inv_five)


def permanent(xi, ai, gi, xj, qj, aj, gj, keep, period):
    delta, inv_three, inv_five = geometry(xi, ai, gi, xj, aj, gj, keep, period)
    return jnp.sum(delta * (inv_three * qj[None, :])[None], axis=-1)


def mutual(xi, ai, gi, xj, aj, gj, muj, keep, period):
    delta, inv_three, inv_five = geometry(xi, ai, gi, xj, aj, gj, keep, period)
    along = jnp.sum(delta * muj[:, :, None, :], axis=0)
    return jnp.sum(delta * (inv_five * along)[None], axis=-1) - jnp.sum(
        inv_three[None] * muj[:, :, None, :], axis=-1
    )


def energy(xi, xj, ai, gi, qj, aj, gj, mui, muj, keep, period):
    first = permanent(xi, ai, gi, xj, qj, aj, gj, keep, period)
    second = mutual(xi, ai, gi, xj, aj, gj, muj, keep, period)
    return -jnp.sum(mui * (first + 0.5 * second))


def neighbour_dipoles(mu, width):
    return extended(mu, (("space", 2),), width)


def per_device(centroids, offsets, velocities, charges, polar, masses, groups, tiles):
    nspace = lax.axis_size("space")
    slab = lax.axis_index("space").astype(jnp.float32)
    atoms_dev = centroids.shape[1]
    beads_dev = offsets.shape[1]
    nblk = atoms_dev // BLOCK
    base = jnp.stack(
        [(slab + centroids[0]) * slab_width, centroids[1] * box_side, centroids[2] * box_side]
    )
    positions = base[:, None, :] + offsets
    props = jnp.stack([charges, polar, groups.astype(jnp.float32)])[:, None, :]
    ext_pos, ext_props = (
        extended(positions, (("space", 2),), atoms_dev),
        extended(props, (("space", 2),), atoms_dev),
    )
    period = jnp.array([nspace * slab_width, box_side, box_side], jnp.float32).reshape(3, 1, 1, 1)
    keep = jnp.ones((NT * BLOCK,), jnp.float32)
    pos_b = positions.reshape(3, beads_dev, nblk, BLOCK)
    ext_b = ext_pos.reshape(3, beads_dev, 3 * nblk, BLOCK)
    ext_q = ext_props[0, 0].reshape(3 * nblk, BLOCK)
    ext_a = ext_props[1, 0].reshape(3 * nblk, BLOCK)
    ext_g = ext_props[2, 0].reshape(3 * nblk, BLOCK)
    own_a = polar.reshape(nblk, BLOCK)
    own_g = ext_g[nblk : 2 * nblk]
    order = jnp.arange(nblk, dtype=jnp.int32)

    def spread(field):
        return jnp.moveaxis(field, 0, 2).reshape(3, -1, atoms_dev)

    def perm_block(b):
        src = tiles[b]
        return permanent(
            pos_b[:, :, b],
            own_a[b],
            own_g[b],
            ext_b[:, :, src].reshape(3, beads_dev, -1),
            ext_q[src].reshape(-1),
            ext_a[src].reshape(-1),
            ext_g[src].reshape(-1),
            keep,
            period,
        )

    field0 = spread(lax.map(perm_block, order))
    mu = polar * field0
    for step in range(ITERS):
        count = beads_dev - 0
        mu_b = neighbour_dipoles(mu, atoms_dev).reshape(3, count, 3 * nblk, BLOCK)

        def one(b):
            src = tiles[b]
            return mutual(
                pos_b[:, :, b],
                own_a[b],
                own_g[b],
                ext_b[:, :, src].reshape(3, count, -1),
                ext_a[src].reshape(-1),
                ext_g[src].reshape(-1),
                mu_b[:, :, src].reshape(3, count, -1),
                keep,
                period,
            )

        mu = polar * (field0 + spread(lax.map(one, order)))
    ext_mu = neighbour_dipoles(mu, atoms_dev)
    ext_mu = ext_mu.reshape(3, beads_dev, 3 * nblk, BLOCK)
    slope = jax.grad(energy, argnums=(0, 1))

    def grad_block(b):
        src = tiles[b]
        return slope(
            pos_b[:, :, b],
            ext_b[:, :, src].reshape(3, beads_dev, -1),
            own_a[b],
            own_g[b],
            ext_q[src].reshape(-1),
            ext_a[src].reshape(-1),
            ext_g[src].reshape(-1),
            ext_mu[:, :, nblk + b],
            ext_mu[:, :, src].reshape(3, beads_dev, -1),
            keep,
            period,
        )

    own_grad, src_grad = lax.map(grad_block, order)
    onehot = (tiles[:, :, None] == jnp.arange(3 * nblk, dtype=jnp.int32)[None, None, :]).astype(
        jnp.float32
    )
    src_grad = src_grad.reshape(nblk, 3, beads_dev, NT, BLOCK)
    ext_grad = jnp.einsum("ncbtl,nte->cbel", src_grad, onehot, precision=lax.Precision.HIGHEST)
    total = jnp.moveaxis(own_grad, 0, 2) + ext_grad[:, :, nblk : 2 * nblk]
    total = total.reshape(3, beads_dev, atoms_dev)
    left_part = ext_grad[:, :, :nblk].reshape(3, beads_dev, atoms_dev)
    right_part = ext_grad[:, :, 2 * nblk :].reshape(3, beads_dev, atoms_dev)
    total = total + shifted(left_part, "space", -1)
    total = total + shifted(right_part, "space", 1)
    forces = -total
    kinetic_sum = lax.psum(
        jnp.sum(masses[None, None, :] * velocities * velocities), ("space", "bead")
    )
    kinetic = kinetic_sum / (3.0 * atoms_dev * nspace * beads_dev * lax.axis_size("bead"))
    scale = jnp.sqrt(1.0 + coupling * (target_temp / kinetic - 1.0))
    padded_beads = extended(offsets, (("bead", 1),), 1)
    before = padded_beads[:, :-2]
    after = padded_beads[:, 2:]
    restoring = -bond_coef * (2.0 * offsets - before - after)
    new_velocity = scale * velocities + time_step * (forces / masses[None, None, :] + restoring)
    new_offset = offsets + time_step * new_velocity
    return (mu, forces, new_velocity, new_offset)


def solution(mesh):
    placed = (
        P(None, "space"),
        P(None, "bead", "space"),
        P(None, "bead", "space"),
        P("space"),
        P("space"),
        P("space"),
        P("space"),
        P("space", None),
    )
    return jax.shard_map(
        per_device,
        mesh=mesh,
        in_specs=placed,
        out_specs=(
            P(None, "bead", "space"),
            P(None, "bead", "space"),
            P(None, "bead", "space"),
            P(None, "bead", "space"),
        ),
        check_vma=False,
    )
```

profile of v0, /device:TPU:1, one launch (start us, length us, event | category | flops | bytes accessed | tf_op | source)
XLA Modules:
  0.0 327.3 jit_solution(9301650586048079981)
XLA Ops:
  2.2 5.4 %collective-permute-start = (f32[3,4,256]{2,1,0:T(4,128)S(1)}, f32[3,4,256]{2,1,0:T(4,128)S(1)}, u32[]{:S(2)}, u32[]{:S(2)}) collective-permute-start(f32[3,4,256]{2,1,0:T(4,128)S(1)} %broadcast_add_fusion), channel_id=1, source_target_pairs={{0,8},{8,16},{16,24},{24,32},{32,40},{40,48},{48,56},{56,64},{64,7... | collective-permute-start | bytes 36872 | tf_op jit(solution)/shard_map/ppermute | solution.py:28
  7.6 5.3 %collective-permute-start.1 = (f32[3,4,256]{2,1,0:T(4,128)S(1)}, f32[3,4,256]{2,1,0:T(4,128)S(1)}, u32[]{:S(2)}, u32[]{:S(2)}) collective-permute-start(f32[3,4,256]{2,1,0:T(4,128)S(1)} %broadcast_add_fusion), channel_id=1, source_target_pairs={{8,0},{16,8},{24,16},{32,24},{40,32},{48,40},{56,48},{64,56},{72,6... | collective-permute-start | bytes 36872 | tf_op jit(solution)/shard_map/ppermute | solution.py:29
  16.2 8.7 %collective-permute-start.3 = (f32[3,1,256]{2,1,0:T(1,128)S(1)}, f32[3,1,256]{2,1,0:T(1,128)S(1)}, u32[]{:S(2)}, u32[]{:S(2)}) collective-permute-start(f32[3,1,256]{2,1,0:T(1,128)S(1)} %broadcast_in_dim.161), channel_id=1, source_target_pairs={{8,0},{16,8},{24,16},{32,24},{40,32},{48,40},{56,48},{64,56},{72,6... | collective-permute-start | bytes 9224 | tf_op jit(solution)/shard_map/ppermute | solution.py:29
  25.8 19.4 %while.59 = (s32[]{:T(128)}, f32[2,3,4,128]{3,2,1,0:T(4,128)S(1)}, s32[2]{0:T(128)S(1)}, f32[3,4,2,128]{3,1,0,2:T(4,128)S(1)}, s32[2,4]{1,0:T(2,128)}, /*index=5...) while((s32[]{:T(128)}, f32[2,3,4,128]{3,2,1,0:T(4,128)S(1)}, ...), condition=%wide.region_3.4_spmd.clone, body=%wide.region_0.3_spmd.clone.sunk | while | flops 16711185 | bytes 5463591 | solution.py:120
  47.8 8.4 %collective-permute-start.5 = (f32[3,4,256]{2,1,0:T(4,128)S(1)}, f32[3,4,256]{2,1,0:T(4,128)S(1)}, u32[]{:S(2)}, u32[]{:S(2)}) collective-permute-start(f32[3,4,256]{2,1,0:T(4,128)S(1)} %bitcast_multiply_fusion), channel_id=1, source_target_pairs={{8,0},{16,8},{24,16},{32,24},{40,32},{48,40},{56,48},{64,56},{72,6... | collective-permute-start | bytes 36872 | tf_op jit(solution)/shard_map/ppermute | solution.py:29
  57.0 21.8 %while.60 = (s32[]{:T(128)}, f32[2,3,4,128]{3,2,1,0:T(4,128)S(1)}, s32[2]{0:T(128)S(1)}, f32[3,4,2,128]{3,1,0,2:T(4,128)S(1)}, s32[2,4]{1,0:T(2,128)}, /*index=5...) while((s32[]{:T(128)}, f32[2,3,4,128]{3,2,1,0:T(4,128)S(1)}, ...), condition=%wide.region_9.10_spmd.clone, body=%wide.region_4.9_spmd.clone.sunk | while | flops 21691920 | bytes 9811495 | solution.py:140
  61.5 1.9 fusion.196
  81.5 8.6 %collective-permute-start.7 = (f32[3,4,256]{2,1,0:T(4,128)S(1)}, f32[3,4,256]{2,1,0:T(4,128)S(1)}, u32[]{:S(2)}, u32[]{:S(2)}) collective-permute-start(f32[3,4,256]{2,1,0:T(4,128)S(1)} %fusion.122), channel_id=1, source_target_pairs={{8,0},{16,8},{24,16},{32,24},{40,32},{48,40},{56,48},{64,56},{72,6... | collective-permute-start | bytes 36872 | tf_op jit(solution)/shard_map/ppermute | solution.py:29
  90.8 21.8 %while.61 = (s32[]{:T(128)}, f32[2,3,4,128]{3,2,1,0:T(4,128)S(1)}, s32[2]{0:T(128)S(1)}, f32[3,4,2,128]{3,1,0,2:T(4,128)S(1)}, s32[2,4]{1,0:T(2,128)}, /*index=5...) while((s32[]{:T(128)}, f32[2,3,4,128]{3,2,1,0:T(4,128)S(1)}, ...), condition=%wide.region_15.16_spmd.clone, body=%wide.region_10.15_spmd.clone.sunk | while | flops 21691920 | bytes 9811495 | solution.py:140
  95.2 1.9 fusion.203
  115.2 8.4 %collective-permute-start.9 = (f32[3,4,256]{2,1,0:T(4,128)S(1)}, f32[3,4,256]{2,1,0:T(4,128)S(1)}, u32[]{:S(2)}, u32[]{:S(2)}) collective-permute-start(f32[3,4,256]{2,1,0:T(4,128)S(1)} %fusion.121), channel_id=1, source_target_pairs={{8,0},{16,8},{24,16},{32,24},{40,32},{48,40},{56,48},{64,56},{72,6... | collective-permute-start | bytes 36872 | tf_op jit(solution)/shard_map/ppermute | solution.py:29
  124.5 21.8 %while.62 = (s32[]{:T(128)}, f32[2,3,4,128]{3,2,1,0:T(4,128)S(1)}, s32[2]{0:T(128)S(1)}, f32[3,4,2,128]{3,1,0,2:T(4,128)S(1)}, s32[2,4]{1,0:T(2,128)}, /*index=5...) while((s32[]{:T(128)}, f32[2,3,4,128]{3,2,1,0:T(4,128)S(1)}, ...), condition=%wide.region_21.22_spmd.clone, body=%wide.region_16.21_spmd.clone.sunk | while | flops 21691920 | bytes 9811495 | solution.py:140
  149.0 8.4 %collective-permute-start.11 = (f32[3,4,256]{2,1,0:T(4,128)S(1)}, f32[3,4,256]{2,1,0:T(4,128)S(1)}, u32[]{:S(2)}, u32[]{:S(2)}) collective-permute-start(f32[3,4,256]{2,1,0:T(4,128)S(1)} %fusion.120), channel_id=1, source_target_pairs={{8,0},{16,8},{24,16},{32,24},{40,32},{48,40},{56,48},{64,56},{72,6... | collective-permute-start | bytes 36872 | tf_op jit(solution)/shard_map/ppermute | solution.py:29
  158.0 3.1 collective-permute-start.14
  161.1 4.5 %collective-permute-start.15 = (f32[3,1,256]{2,1,0:T(1,128)}, f32[3,1,256]{2,1,0:T(1,128)}, u32[]{:S(2)}, u32[]{:S(2)}) collective-permute-start(f32[3,1,256]{2,1,0:T(1,128)} %get-tuple-element.955), channel_id=1, source_target_pairs={{1,0},{2,1},{3,2},{4,3},{5,4},{6,5},{7,6},{0,7},{9,8},{10,9},{11,1... | collective-permute-start | bytes 9224 | tf_op jit(solution)/shard_map/ppermute | solution.py:29
  166.2 47.7 %while.63 = (s32[]{:T(128)}, f32[2,3,4,128]{3,0,2,1:T(2,128)}, f32[2,3,4,512]{3,2,1,0:T(4,128)}, s32[2]{0:T(128)}, f32[3,4,6,128]{3,1,2,0:T(4,128)S(1)}, /*index...) while((s32[]{:T(128)}, f32[2,3,4,128]{3,0,2,1:T(2,128)}, ...), condition=%wide.region_32.33_spmd.clone, body=%wide.region_22.32_spmd.clone.sunk | while | flops 64432148 | bytes 27084660 | solution.py:161
  172.2 3.9 %fusion.218 = (f32[4,128,512]{2,1,0:T(8,128)S(1)}, f32[4,128,512]{2,1,0:T(8,128)S(1)}, f32[4,128,512]{2,1,0:T(8,128)S(1)}, f32[4,128,512]{2,1,0:T(8,128)}) fusion(f32[3]{0:T(128)} %get-tuple-element.1644, f32[3]{0:T(128)} %get-tuple-element.1645, f32[3,4,512]{2,1,0:T(4,128)S(1)} %get-tuple-element.1380, ...), kind=kLoop, calls=%fused_computation.179.clone.1 | loop fusion | flops 9961472 | bytes 4261912 | tf_op jit(solution)/shard_map/while/body/eval_jaxpr/jvp()/reduce_sum | solution.py:42
  177.5 4.2 %fusion.220 = (f32[4,128,512]{2,1,0:T(8,128)S(1)}, f32[4,128,512]{2,1,0:T(8,128)S(1)}, f32[4,128,512]{2,1,0:T(8,128)S(1)}) fusion(f32[4,128,512]{2,1,0:T(8,128)S(1)} %get-tuple-element.1384, f32[128,512]{1,0:T(8,128)S(1)} %multiply_sqrt_fusion.14, f32[128,512]{1,0:T(8,128)S(1)} %compare_select_fusion.19, f32[4,128,512]{2,1,0:T(8,128)S(1)} %get-tuple-element.1387, ...), kind=kLoop, calls=%fused_computation.239.clone.1 | loop fusion | flops 20185088 | bytes 7864320 | tf_op jit(solution)/shard_map/while/body/eval_jaxpr/jvp()/mul | solution.py:62
  182.5 2.4 fusion.221
  196.1 3.9 %fusion.218 = (f32[4,128,512]{2,1,0:T(8,128)S(1)}, f32[4,128,512]{2,1,0:T(8,128)S(1)}, f32[4,128,512]{2,1,0:T(8,128)S(1)}, f32[4,128,512]{2,1,0:T(8,128)}) fusion(f32[3]{0:T(128)} %get-tuple-element.1644, f32[3]{0:T(128)} %get-tuple-element.1645, f32[3,4,512]{2,1,0:T(4,128)S(1)} %get-tuple-element.1380, ...), kind=kLoop, calls=%fused_computation.179.clone.1 | loop fusion | flops 9961472 | bytes 4261912 | tf_op jit(solution)/shard_map/while/body/eval_jaxpr/jvp()/reduce_sum | solution.py:42
  201.4 4.2 %fusion.220 = (f32[4,128,512]{2,1,0:T(8,128)S(1)}, f32[4,128,512]{2,1,0:T(8,128)S(1)}, f32[4,128,512]{2,1,0:T(8,128)S(1)}) fusion(f32[4,128,512]{2,1,0:T(8,128)S(1)} %get-tuple-element.1384, f32[128,512]{1,0:T(8,128)S(1)} %multiply_sqrt_fusion.14, f32[128,512]{1,0:T(8,128)S(1)} %compare_select_fusion.19, f32[4,128,512]{2,1,0:T(8,128)S(1)} %get-tuple-element.1387, ...), kind=kLoop, calls=%fused_computation.239.clone.1 | loop fusion | flops 20185088 | bytes 7864320 | tf_op jit(solution)/shard_map/while/body/eval_jaxpr/jvp()/mul | solution.py:62
  206.3 2.4 fusion.221
  216.5 8.4 %collective-permute-start.12 = (f32[3,4,256]{2,1,0:T(4,128)S(1)}, f32[3,4,256]{2,1,0:T(4,128)S(1)}, u32[]{:S(2)}, u32[]{:S(2)}) collective-permute-start(f32[3,4,256]{2,1,0:T(4,128)S(1)} %reshape.868), channel_id=1, source_target_pairs={{0,504},{8,0},{16,8},{24,16},{32,24},{40,32},{48,40},{56,48},{64,5... | collective-permute-start | bytes 36872 | tf_op jit(solution)/shard_map/ppermute | solution.py:36
  228.2 96.9 %psum.7 = f32[]{:T(128)} all-reduce(f32[]{:T(128)} %fusion.119), channel_id=1, replica_groups=mesh['space'=64,'bead'=8] {'space','bead'}, use_global_device_ids=true, to_apply=%region_34.35 | all-reduce | flops 1 | bytes 8 | tf_op jit(solution)/shard_map/psum | solution.py:174
  (331 shorter events, 112.1 us)
Async XLA Ops:
  2.2 23.6 %collective-permute-start = (f32[3,4,256]{2,1,0:T(4,128)S(1)}, f32[3,4,256]{2,1,0:T(4,128)S(1)}, u32[]{:S(2)}, u32[]{:S(2)}) collective-permute-start(f32[3,4,256]{2,1,0:T(4,128)S(1)} %broadcast_add_fusion), channel_id=1, source_target_pairs={{0,8},{8,16},{16,24},{24,32},{32,40},{40,48},{48,56},{56,64},{64,7... | collective-permute-start | bytes 36872 | tf_op jit(solution)/shard_map/ppermute | solution.py:28
  7.6 18.2 %collective-permute-start.1 = (f32[3,4,256]{2,1,0:T(4,128)S(1)}, f32[3,4,256]{2,1,0:T(4,128)S(1)}, u32[]{:S(2)}, u32[]{:S(2)}) collective-permute-start(f32[3,4,256]{2,1,0:T(4,128)S(1)} %broadcast_add_fusion), channel_id=1, source_target_pairs={{8,0},{16,8},{24,16},{32,24},{40,32},{48,40},{56,48},{64,56},{72,6... | collective-permute-start | bytes 36872 | tf_op jit(solution)/shard_map/ppermute | solution.py:29
  14.3 11.4 %collective-permute-start.2 = (f32[3,1,256]{2,1,0:T(1,128)S(1)}, f32[3,1,256]{2,1,0:T(1,128)S(1)}, u32[]{:S(2)}, u32[]{:S(2)}) collective-permute-start(f32[3,1,256]{2,1,0:T(1,128)S(1)} %broadcast_in_dim.161), channel_id=1, source_target_pairs={{0,8},{8,16},{16,24},{24,32},{32,40},{40,48},{48,56},{56,64},{64,7... | collective-permute-start | bytes 9224 | tf_op jit(solution)/shard_map/ppermute | solution.py:28
  16.2 9.5 %collective-permute-start.3 = (f32[3,1,256]{2,1,0:T(1,128)S(1)}, f32[3,1,256]{2,1,0:T(1,128)S(1)}, u32[]{:S(2)}, u32[]{:S(2)}) collective-permute-start(f32[3,1,256]{2,1,0:T(1,128)S(1)} %broadcast_in_dim.161), channel_id=1, source_target_pairs={{8,0},{16,8},{24,16},{32,24},{40,32},{48,40},{56,48},{64,56},{72,6... | collective-permute-start | bytes 9224 | tf_op jit(solution)/shard_map/ppermute | solution.py:29
  25.8 6.1 %copy-start.14 = (f32[2,128]{1,0:T(2,128)S(1)}, f32[2,128]{1,0:T(2,128)}, u32[]{:S(2)}) copy-start(f32[2,128]{1,0:T(2,128)} %get-tuple-element.1440) | copy-start | bytes 3076 | tf_op jit(solution)/shard_map/while
  35.5 6.1 %copy-start.14 = (f32[2,128]{1,0:T(2,128)S(1)}, f32[2,128]{1,0:T(2,128)}, u32[]{:S(2)}) copy-start(f32[2,128]{1,0:T(2,128)} %get-tuple-element.1440) | copy-start | bytes 3076 | tf_op jit(solution)/shard_map/while
  45.9 10.3 %collective-permute-start.4 = (f32[3,4,256]{2,1,0:T(4,128)S(1)}, f32[3,4,256]{2,1,0:T(4,128)S(1)}, u32[]{:S(2)}, u32[]{:S(2)}) collective-permute-start(f32[3,4,256]{2,1,0:T(4,128)S(1)} %bitcast_multiply_fusion), channel_id=1, source_target_pairs={{0,8},{8,16},{16,24},{24,32},{32,40},{40,48},{48,56},{56,64},{64,7... | collective-permute-start | bytes 36872 | tf_op jit(solution)/shard_map/ppermute | solution.py:28
  47.8 9.2 %collective-permute-start.5 = (f32[3,4,256]{2,1,0:T(4,128)S(1)}, f32[3,4,256]{2,1,0:T(4,128)S(1)}, u32[]{:S(2)}, u32[]{:S(2)}) collective-permute-start(f32[3,4,256]{2,1,0:T(4,128)S(1)} %bitcast_multiply_fusion), channel_id=1, source_target_pairs={{8,0},{16,8},{24,16},{32,24},{40,32},{48,40},{56,48},{64,56},{72,6... | collective-permute-start | bytes 36872 | tf_op jit(solution)/shard_map/ppermute | solution.py:29
  79.6 10.5 %collective-permute-start.6 = (f32[3,4,256]{2,1,0:T(4,128)S(1)}, f32[3,4,256]{2,1,0:T(4,128)S(1)}, u32[]{:S(2)}, u32[]{:S(2)}) collective-permute-start(f32[3,4,256]{2,1,0:T(4,128)S(1)} %fusion.122), channel_id=1, source_target_pairs={{0,8},{8,16},{16,24},{24,32},{32,40},{40,48},{48,56},{56,64},{64,7... | collective-permute-start | bytes 36872 | tf_op jit(solution)/shard_map/ppermute | solution.py:28
  81.5 9.3 %collective-permute-start.7 = (f32[3,4,256]{2,1,0:T(4,128)S(1)}, f32[3,4,256]{2,1,0:T(4,128)S(1)}, u32[]{:S(2)}, u32[]{:S(2)}) collective-permute-start(f32[3,4,256]{2,1,0:T(4,128)S(1)} %fusion.122), channel_id=1, source_target_pairs={{8,0},{16,8},{24,16},{32,24},{40,32},{48,40},{56,48},{64,56},{72,6... | collective-permute-start | bytes 36872 | tf_op jit(solution)/shard_map/ppermute | solution.py:29
  113.3 10.4 %collective-permute-start.8 = (f32[3,4,256]{2,1,0:T(4,128)S(1)}, f32[3,4,256]{2,1,0:T(4,128)S(1)}, u32[]{:S(2)}, u32[]{:S(2)}) collective-permute-start(f32[3,4,256]{2,1,0:T(4,128)S(1)} %fusion.121), channel_id=1, source_target_pairs={{0,8},{8,16},{16,24},{24,32},{32,40},{40,48},{48,56},{56,64},{64,7... | collective-permute-start | bytes 36872 | tf_op jit(solution)/shard_map/ppermute | solution.py:28
  115.2 9.3 %collective-permute-start.9 = (f32[3,4,256]{2,1,0:T(4,128)S(1)}, f32[3,4,256]{2,1,0:T(4,128)S(1)}, u32[]{:S(2)}, u32[]{:S(2)}) collective-permute-start(f32[3,4,256]{2,1,0:T(4,128)S(1)} %fusion.121), channel_id=1, source_target_pairs={{8,0},{16,8},{24,16},{32,24},{40,32},{48,40},{56,48},{64,56},{72,6... | collective-permute-start | bytes 36872 | tf_op jit(solution)/shard_map/ppermute | solution.py:29
  124.5 32.9 %copy-start.19 = (f32[3,4,256]{2,1,0:T(4,128)S(1)}, f32[3,4,256]{2,1,0:T(4,128)}, u32[]{:S(2)}) copy-start(f32[3,4,256]{2,1,0:T(4,128)} %param.20) | copy-start | bytes 36868
  147.1 19.2 %copy-start.22 = (f32[3,4,256]{2,1,0:T(4,128)}, f32[3,4,256]{2,1,0:T(4,128)S(1)}, u32[]{:S(2)}) copy-start(f32[3,4,256]{2,1,0:T(4,128)S(1)} %fusion.120) | copy-start | bytes 36868
  147.1 18.6 %collective-permute-start.10 = (f32[3,4,256]{2,1,0:T(4,128)S(1)}, f32[3,4,256]{2,1,0:T(4,128)S(1)}, u32[]{:S(2)}, u32[]{:S(2)}) collective-permute-start(f32[3,4,256]{2,1,0:T(4,128)S(1)} %fusion.120), channel_id=1, source_target_pairs={{0,8},{8,16},{16,24},{24,32},{32,40},{40,48},{48,56},{56,64},{64,7... | collective-permute-start | bytes 36872 | tf_op jit(solution)/shard_map/ppermute | solution.py:28
  149.0 16.7 %collective-permute-start.11 = (f32[3,4,256]{2,1,0:T(4,128)S(1)}, f32[3,4,256]{2,1,0:T(4,128)S(1)}, u32[]{:S(2)}, u32[]{:S(2)}) collective-permute-start(f32[3,4,256]{2,1,0:T(4,128)S(1)} %fusion.120), channel_id=1, source_target_pairs={{8,0},{16,8},{24,16},{32,24},{40,32},{48,40},{56,48},{64,56},{72,6... | collective-permute-start | bytes 36872 | tf_op jit(solution)/shard_map/ppermute | solution.py:29
  158.0 167.8 %collective-permute-start.14 = (f32[3,1,256]{2,1,0:T(1,128)}, f32[3,1,256]{2,1,0:T(1,128)}, u32[]{:S(2)}, u32[]{:S(2)}) collective-permute-start(f32[3,1,256]{2,1,0:T(1,128)} %get-tuple-element.954), channel_id=1, source_target_pairs={{0,1},{1,2},{2,3},{3,4},{4,5},{5,6},{6,7},{7,0},{8,9},{9,10},{10,1... | collective-permute-start | bytes 9224 | tf_op jit(solution)/shard_map/ppermute | solution.py:28
  161.1 164.7 %collective-permute-start.15 = (f32[3,1,256]{2,1,0:T(1,128)}, f32[3,1,256]{2,1,0:T(1,128)}, u32[]{:S(2)}, u32[]{:S(2)}) collective-permute-start(f32[3,1,256]{2,1,0:T(1,128)} %get-tuple-element.955), channel_id=1, source_target_pairs={{1,0},{2,1},{3,2},{4,3},{5,4},{6,5},{7,6},{0,7},{9,8},{10,9},{11,1... | collective-permute-start | bytes 9224 | tf_op jit(solution)/shard_map/ppermute | solution.py:29
  166.2 6.0 %copy-start.12 = (f32[3,4,6,128]{3,1,2,0:T(4,128)}, f32[3,4,6,128]{3,1,2,0:T(4,128)S(1)}, u32[]{:S(2)}) copy-start(f32[3,4,6,128]{3,1,2,0:T(4,128)S(1)} %get-tuple-element.1634) | copy-start | bytes 110596 | tf_op jit(solution)/shard_map/while
  177.5 4.9 %copy-start.6 = (f32[3]{0:T(128)S(1)}, f32[3]{0:T(128)}, u32[]{:S(2)}) copy-start(f32[3]{0:T(128)} %get-tuple-element.1644) | copy-start | bytes 40 | tf_op jit(solution)/shard_map/while
  190.1 6.0 %copy-start.12 = (f32[3,4,6,128]{3,1,2,0:T(4,128)}, f32[3,4,6,128]{3,1,2,0:T(4,128)S(1)}, u32[]{:S(2)}) copy-start(f32[3,4,6,128]{3,1,2,0:T(4,128)S(1)} %get-tuple-element.1634) | copy-start | bytes 110596 | tf_op jit(solution)/shard_map/while
  201.4 4.9 %copy-start.6 = (f32[3]{0:T(128)S(1)}, f32[3]{0:T(128)}, u32[]{:S(2)}) copy-start(f32[3]{0:T(128)} %get-tuple-element.1644) | copy-start | bytes 40 | tf_op jit(solution)/shard_map/while
  216.5 109.4 %collective-permute-start.12 = (f32[3,4,256]{2,1,0:T(4,128)S(1)}, f32[3,4,256]{2,1,0:T(4,128)S(1)}, u32[]{:S(2)}, u32[]{:S(2)}) collective-permute-start(f32[3,4,256]{2,1,0:T(4,128)S(1)} %reshape.868), channel_id=1, source_target_pairs={{0,504},{8,0},{16,8},{24,16},{32,24},{40,32},{48,40},{56,48},{64,5... | collective-permute-start | bytes 36872 | tf_op jit(solution)/shard_map/ppermute | solution.py:36
  224.9 100.9 %collective-permute-start.13 = (f32[3,4,256]{2,1,0:T(4,128)S(1)}, f32[3,4,256]{2,1,0:T(4,128)S(1)}, u32[]{:S(2)}, u32[]{:S(2)}) collective-permute-start(f32[3,4,256]{2,1,0:T(4,128)S(1)} %reshape.869), channel_id=1, source_target_pairs={{0,8},{8,16},{16,24},{24,32},{32,40},{40,48},{48,56},{56,64},{64,7... | collective-permute-start | bytes 36872 | tf_op jit(solution)/shard_map/ppermute | solution.py:36
  (40 other events, 75.6 us)
where the time goes:
time: 329 us; the launch traced here: 327 us
  blocking collectives  96.9 us (29%)
  other arithmetic  85.1 us (26%)
  starting transfers between devices  80.7 us (25%)
  local copies, waits for them, and re-layouts  37.1 us (11%)
  loops' own time  22.4 us (7%)
    psum x1, blocking collectives, per_device(): lax.psum(jnp.sum(masses[None, None, :] * velocities * velocities), ('spac...  96.9 us
    ppermute x7, starting transfers between devices, extended(): after = lax.ppermute(first, axis, down)  52.4 us
    reduce_sum x10, other arithmetic, geometry(): square = jnp.sum(delta * delta, axis=0) + 1.0  22.7 us
    ppermute x7, starting transfers between devices, extended(): before = lax.ppermute(last, axis, up)  18 us
    another operation x3, loops' own time, per_device(): mu = polar * (field0 + spread(lax.map(one, order)))  12.3 us
    ppermute x2, starting transfers between devices, shifted(): lax.ppermute(array, axis, [(i, (i + by) % count) for i in range(count)])  10.3 us
    reduce_sum x4, other arithmetic, geometry(): delta = xi[:, :, :, None] - xj[:, :, None, :]  8.7 us
    mul x2, other arithmetic, mutual(): inv_five * along  8.35 us
  transfers between devices with their start and end apart: 16, of which 4 were waited for; matrix products, arithmetic and copies ran while one was open for 15% of the time, Pallas kernels for 0%

commit v1 on v0

v1 whole, which is shorter than its diff:
```python
import functools

import jax
import jax.numpy as jnp
from jax import lax
from jax.experimental import pallas as pl
from jax.experimental.pallas import tpu as pltpu
from jax.sharding import Mesh
from jax.sharding import PartitionSpec as P

BLOCK = 128
NT = 4
ITERS = 3
GROUP = 4
ROW = 16
HALO = 5
WINDOW = GROUP + 2 * HALO
WBLK = 2 * WINDOW
KEPT = 2 * (WINDOW - 4)

slab_width = 9.0
box_side = 24.0
cut_square = 64.0
thole_coef = 0.39
bond_coef = 4.0
time_step = 0.05
target_temp = 8.0
coupling = 0.5

F32 = jnp.float32
I32 = jnp.int32
UNIT = 2.0**-12
STEPS = 2.0**32 / box_side
VMEM = pl.BlockSpec(memory_space=pltpu.VMEM)
SMEM = pl.BlockSpec(memory_space=pltpu.SMEM)


def pack_kernel(slab_ref, tiles_ref, cen_ref, off_ref, vel_ref, q_ref, a_ref, m_ref, g_ref, out_ref):
    slab = slab_ref[0].astype(F32)
    bx = (slab + cen_ref[0:1, :]) * slab_width
    by = cen_ref[1:2, :] * box_side
    bz = cen_ref[2:3, :] * box_side
    lane = lax.broadcasted_iota(I32, (1, 256), 1)
    marks = jnp.zeros((1, 256), F32)
    for b in range(2):
        for t in range(NT):
            marks = jnp.where(lane == b * NT + t, tiles_ref[b, t].astype(F32), marks)
    v = vel_ref[...]
    kin = jnp.sum(m_ref[...] * jnp.sum(v * v, axis=(0, 1))[None, :], axis=1, keepdims=True)
    kin = jnp.broadcast_to(kin, (1, 256))
    for r in range(4):
        rows = jnp.concatenate(
            [
                bx + off_ref[0, r : r + 1, :],
                by + off_ref[1, r : r + 1, :],
                bz + off_ref[2, r : r + 1, :],
                q_ref[...],
                a_ref[...],
                g_ref[...].astype(F32),
                marks,
                kin,
            ],
            axis=0,
        )
        for d in range(ROW // GROUP):
            out_ref[d * GROUP + r] = rows


def column(tile, c):
    return jnp.broadcast_to(tile[:, c : c + 1], (8, BLOCK))


def rows_of(acc):
    ones = jnp.ones((8, BLOCK), F32)
    return lax.dot_general(
        ones, acc, (((1,), (1,)), ((), ())), precision=lax.Precision.HIGHEST, preferred_element_type=F32
    )


def distances(ci, cj, kf, ki):
    dx = column(kf, 0) - ci[0]
    dy = (ki[0] - cj[0]).astype(F32) * (1.0 / STEPS)
    dz = (ki[1] - cj[1]).astype(F32) * (1.0 / STEPS)
    return dx, dy, dz


def main_kernel(
    place_ref, v_ref, h_ref, out_ref, srcf, srci, colf, coli, marks_v, marks, pair, acc, field, mu_a, mu_b, sem
):
    grp = place_ref[0]
    row = place_ref[1]
    line = lax.broadcasted_iota(I32, (8, BLOCK), 0)

    def load_slab(w, carry):
        r = grp * GROUP - HALO + w
        inside = jnp.logical_and(r >= 0, r < ROW)
        far = jnp.where(r < 0, r + HALO, r - ROW)
        slab = row * ROW + r
        shift = jnp.where(slab < 0, -576.0, jnp.where(slab >= 64, 576.0, 0.0)).astype(F32)
        whole = jnp.where(inside, v_ref[jnp.clip(r, 0, ROW - 1)], h_ref[jnp.clip(far, 0, HALO - 1)])
        marks_v[pl.ds(w, 1), :] = whole[6:7, :BLOCK].astype(I32)
        for half in range(2):
            blk = 2 * w + half
            d = whole[:, half * BLOCK : (half + 1) * BLOCK]
            wrapped = d - box_side * jnp.floor(d * (1.0 / box_side) + 0.5)
            fixed = jnp.clip(wrapped * STEPS, -2147483648.0, 2147483520.0).astype(I32)
            d = jnp.where(line == 0, d + shift, d)
            d = jnp.where(line == 7, thole_coef**0.5 * lax.rsqrt(d[4:5]), d)
            for n, c in enumerate((0, 3, 7, 5, 4)):
                scale = UNIT if c in (3, 4) else 1.0
                srcf[blk, n] = jnp.broadcast_to(d[c : c + 1] * scale, (8, BLOCK))
            for n in range(2):
                srci[blk, n] = jnp.broadcast_to(fixed[n + 1 : n + 2], (8, BLOCK))
            at = pl.multiple_of(blk * BLOCK, BLOCK)
            colf[pl.ds(at, BLOCK), :] = jnp.transpose(jnp.where(line == 7, -d, d))
            coli[pl.ds(at, BLOCK), :] = jnp.transpose(fixed)
        return carry

    lax.fori_loop(0, WINDOW, load_slab, 0)
    copy = pltpu.make_async_copy(marks_v, marks, sem)
    copy.start()
    copy.wait()

    def source(blk, k):
        w = lax.div(blk, 2)
        return 2 * (w - 1) + marks[w, lax.rem(blk, 2) * NT + k]

    def targets(i, blk):
        at = pl.multiple_of(blk * BLOCK + i * 8, 8)
        return colf[pl.ds(at, 8), :], coli[pl.ds(at, 8), :]

    def field_block(blk, carry):
        src = [source(blk, k) for k in range(NT)]
        slot = jnp.where(jnp.logical_and(blk >= 4, blk < WBLK - 4), blk - 4, KEPT)

        def tile(i, carry):
            kf, ki = targets(i, blk)
            xi, gi, idi = column(kf, 0), column(kf, 7), column(kf, 5)
            yi, zi = column(ki, 1), column(ki, 2)
            at = pl.multiple_of(i * 8, 8)
            sums = [jnp.zeros((8, BLOCK), F32)] * 3
            for k in range(NT):
                s = src[k]
                dx = xi - srcf[s, 0]
                dy = (yi - srci[s, 0]).astype(F32) * (1.0 / STEPS)
                dz = (zi - srci[s, 1]).astype(F32) * (1.0 / STEPS)
                sq = dx * dx + dy * dy + dz * dz + 1.0
                r = lax.rsqrt(sq)
                gg = jnp.where(idi == srcf[s, 3], 0.0, gi * srcf[s, 2])
                un = gg * sq * (sq * r)
                f = jnp.exp(un)
                l3 = 1.0 - f
                l5 = l3 + un * f
                t = jnp.maximum(cut_square - sq, 0.0)
                r2 = r * r
                tp = t * (t * (r2 * r))
                b3 = tp * l3
                b5 = (3.0 * r2) * tp * l5
                for n, val in enumerate((dx, dy, dz, b3, b5)):
                    pair[slot, k, n, pl.ds(at, 8), :] = val
                w = b3 * srcf[s, 1]
                sums = [sums[0] + w * dx, sums[1] + w * dy, sums[2] + w * dz]
            for n in range(3):
                acc[n, pl.ds(at, 8), :] = sums[n]
            return carry

        lax.fori_loop(0, 16, tile, 0, unroll=2)
        for n in range(3):
            rows = rows_of(acc[n])
            field[blk, n] = rows
            mu_a[blk, n] = srcf[blk, 4] * rows
        return carry

    lax.fori_loop(2, WBLK - 2, field_block, 0)

    def mutual_block(old, new, blk, carry):
        src = [source(blk, k) for k in range(NT)]
        mus = [[old[src[k], n] for n in range(3)] for k in range(NT)]

        def tile(i, carry):
            at = pl.multiple_of(i * 8, 8)
            sums = [jnp.zeros((8, BLOCK), F32)] * 3
            for k in range(NT):
                dx, dy, dz, b3, b5 = [pair[blk - 4, k, n, pl.ds(at, 8), :] for n in range(5)]
                mx, my, mz = mus[k]
                w = b5 * (dx * mx + dy * my + dz * mz)
                sums = [
                    sums[0] + (w * dx - b3 * mx),
                    sums[1] + (w * dy - b3 * my),
                    sums[2] + (w * dz - b3 * mz),
                ]
            for n in range(3):
                acc[n, pl.ds(at, 8), :] = sums[n]
            return carry

        lax.fori_loop(0, 16, tile, 0, unroll=4)
        for n in range(3):
            new[blk, n] = srcf[blk, 4] * (field[blk, n] + rows_of(acc[n]))
        return carry

    old, new = mu_a, mu_b
    for step in range(ITERS):
        edge = 4 + 2 * step
        lax.fori_loop(edge, WBLK - edge, functools.partial(mutual_block, old, new), 0)
        old, new = new, old
    mu = old

    def force_block(n_own, carry):
        blk = 2 * HALO + n_own
        w = lax.div(blk, 2)
        first = 2 * (w - 1)
        a_of, b_of, c_of = [], [], []
        for c in range(6):
            s = first + c
            ws = lax.div(s, 2)
            here = jnp.float32(0.0)
            there = jnp.float32(0.0)
            for k in range(NT):
                here = here + jnp.where(marks[w, lax.rem(blk, 2) * NT + k] == c, 1.0, 0.0).astype(F32)
                there = there + jnp.where(
                    marks[ws, lax.rem(s, 2) * NT + k] == blk - 2 * (ws - 1), 1.0, 0.0
                ).astype(F32)
            a_of.append(here)
            b_of.append(there)
            c_of.append(0.5 * (here + there))
        own = [mu[blk, n] * (1.0 / UNIT) for n in range(3)]
        col = jnp.where(line == 0, own[0], jnp.where(line == 1, own[1], own[2]))
        acc[3, :, 0:8] = jnp.transpose(col)

        def tile(i, carry):
            kf, ki = targets(i, blk)
            at = pl.multiple_of(i * 8, 8)
            km = acc[3, pl.ds(at, 8), 0:8]
            xi, gi, idi, qi = column(kf, 0), column(kf, 7), column(kf, 5), column(kf, 3)
            yi, zi = column(ki, 1), column(ki, 2)
            ax, ay, az = column(km, 0), column(km, 1), column(km, 2)
            fx, fy, fz, along = [jnp.zeros((8, BLOCK), F32)] * 4
            for c in range(6):
                s = first + c
                dx = xi - srcf[s, 0]
                dy = (yi - srci[s, 0]).astype(F32) * (1.0 / STEPS)
                dz = (zi - srci[s, 1]).astype(F32) * (1.0 / STEPS)
                sq = dx * dx + dy * dy + dz * dz + 1.0
                r = lax.rsqrt(sq)
                gg = jnp.where(idi == srcf[s, 3], 0.0, gi * srcf[s, 2])
                un = gg * sq * (sq * r)
                f = jnp.exp(un)
                l3 = 1.0 - f
                unf = un * f
                l5 = l3 + unf
                t = jnp.maximum(cut_square - sq, 0.0)
                r2 = r * r
                p = t * (r2 * r)
                pl3 = p * l3
                b3 = t * pl3
                pr = (3.0 * r2) * p
                b5 = (t * pr) * l5
                k3 = -4.0 * pl3 - b5
                k5 = pr * (t * r2 * (1.5 * (un * unf) - 2.5 * l5) - 2.0 * l5)
                bx, by, bz = mu[s, 0], mu[s, 1], mu[s, 2]
                di = dx * ax + dy * ay + dz * az
                dj = dx * bx + dy * by + dz * bz
                mm = ax * bx + ay * by + az * bz
                qa = a_of[c] * srcf[s, 1]
                qb = b_of[c] * qi
                k2 = k3 * (qa * di - qb * dj - c_of[c] * mm) + (2.0 * c_of[c]) * (k5 * (di * dj))
                h = c_of[c] * b5
                along = along + (qa * b3 + h * dj)
                g = h * di - qb * b3
                fx = fx + (g * bx + k2 * dx)
                fy = fy + (g * by + k2 * dy)
                fz = fz + (g * bz + k2 * dz)
            acc[0, pl.ds(at, 8), :] = fx + along * ax
            acc[1, pl.ds(at, 8), :] = fy + along * ay
            acc[2, pl.ds(at, 8), :] = fz + along * az
            return carry

        lax.fori_loop(0, 16, tile, 0, unroll=2)
        res = jnp.zeros((8, BLOCK), F32)
        for n in range(3):
            res = jnp.where(line == n, own[n], res)
            res = jnp.where(line == n + 3, rows_of(acc[n]), res)
        out_ref[n_own] = res
        return carry

    lax.fori_loop(0, 2 * GROUP, force_block, 0)


def final_kernel(kin_ref, r_ref, off_ref, before_ref, after_ref, vel_ref, m_ref, mu_ref, f_ref, nv_ref, no_ref):
    kinetic = kin_ref[...] * (1.0 / 1572864.0)
    scale = jnp.sqrt(1.0 + coupling * (target_temp / kinetic - 1.0))
    inv = 1.0 / m_ref[...]
    for n in range(3):
        off = off_ref[n]
        before = jnp.concatenate([before_ref[n], off[:3]], axis=0)
        after = jnp.concatenate([off[1:], after_ref[n]], axis=0)
        restoring = -bond_coef * (2.0 * off - before - after)
        mu = jnp.concatenate(
            [jnp.concatenate([r_ref[r, b, n : n + 1, :] for b in range(2)], axis=1) for r in range(4)], axis=0
        )
        force = jnp.concatenate(
            [jnp.concatenate([r_ref[r, b, n + 3 : n + 4, :] for b in range(2)], axis=1) for r in range(4)], axis=0
        )
        mu_ref[n] = mu
        f_ref[n] = force
        nv = scale * vel_ref[n] + time_step * (force * inv + restoring)
        nv_ref[n] = nv
        no_ref[n] = off + time_step * nv


def per_device(centroids, offsets, velocities, charges, polar, masses, groups, tiles):
    yhi, grp, mem = lax.axis_index("yhi"), lax.axis_index("grp"), lax.axis_index("mem")
    slab = ((yhi * 4 + grp) * 4 + mem).astype(I32)
    line = lambda a: a.reshape(1, 256)
    packed = pl.pallas_call(
        pack_kernel,
        out_shape=jax.ShapeDtypeStruct((ROW, 8, 256), F32),
        in_specs=[SMEM, SMEM] + [VMEM] * 7,
        out_specs=VMEM,
        name="pack",
    )(slab.reshape(1), tiles, centroids, offsets, velocities, line(charges), line(polar), line(masses), line(groups))
    got = lax.all_to_all(packed, ("grp", "mem"), split_axis=0, concat_axis=0, tiled=True)
    swap = []
    for y in range(4):
        for i in range(ROW):
            to = (y + (1 if i < ROW // 2 else -1)) % 4
            swap.append((y * ROW + i, to * ROW + i))
    ends = lax.dynamic_slice_in_dim(got, jnp.where(grp < 2, ROW - HALO, 0), HALO, axis=0)
    far = lax.ppermute(ends, ("yhi", "grp", "mem"), swap)

    kin = jnp.sum(got[:, 7, 0])
    kin = lax.psum(lax.psum(kin, "yhi"), "bead")
    up = [(i, (i + 1) % 8) for i in range(8)]
    before = lax.ppermute(offsets[:, 3:], "bead", up)
    after = lax.ppermute(offsets[:, :1], "bead", [(j, i) for i, j in up])

    place = jnp.stack([grp, yhi]).astype(I32)
    done = pl.pallas_call(
        main_kernel,
        out_shape=jax.ShapeDtypeStruct((2 * GROUP, 8, BLOCK), F32),
        in_specs=[SMEM, VMEM, VMEM],
        out_specs=VMEM,
        scratch_shapes=[
            pltpu.VMEM((WBLK, 5, 8, BLOCK), F32),
            pltpu.VMEM((WBLK, 2, 8, BLOCK), I32),
            pltpu.VMEM((WBLK * BLOCK, 8), F32),
            pltpu.VMEM((WBLK * BLOCK, 8), I32),
            pltpu.VMEM((16, BLOCK), I32),
            pltpu.SMEM((16, BLOCK), I32),
            pltpu.VMEM((KEPT + 1, NT, 5, BLOCK, BLOCK), F32),
            pltpu.VMEM((4, BLOCK, BLOCK), F32),
            pltpu.VMEM((WBLK, 3, 8, BLOCK), F32),
            pltpu.VMEM((WBLK, 3, 8, BLOCK), F32),
            pltpu.VMEM((WBLK, 3, 8, BLOCK), F32),
            pltpu.SemaphoreType.DMA,
        ],
        compiler_params=pltpu.CompilerParams(vmem_limit_bytes=50 * 2**20),
        cost_estimate=pl.CostEstimate(flops=400_000_000, bytes_accessed=300_000, transcendentals=0),
        name="dipoles",
    )(place, got, far)
    back = lax.all_to_all(done.reshape(GROUP, 2, 8, BLOCK), "mem", split_axis=0, concat_axis=0, tiled=True)
    shape = jax.ShapeDtypeStruct((3, 4, 256), F32)
    return pl.pallas_call(
        final_kernel,
        out_shape=(shape,) * 4,
        in_specs=[VMEM] * 7,
        out_specs=(VMEM,) * 4,
        name="finish",
    )(kin.reshape(1, 1), back, offsets, before, after, velocities, line(masses))


def solution(mesh):
    fine = Mesh(mesh.devices.reshape(4, 4, 4, 8), ("yhi", "grp", "mem", "bead"))
    space = ("yhi", "grp", "mem")
    placed = (
        P(None, space),
        P(None, "bead", space),
        P(None, "bead", space),
        P(space),
        P(space),
        P(space),
        P(space),
        P(space, None),
    )
    return jax.shard_map(
        per_device,
        mesh=fine,
        in_specs=placed,
        out_specs=(P(None, "bead", space),) * 4,
        check_vma=False,
    )
```

time: 329 us -> 156 us (0.47)
  the two profiles are of different devices: /device:TPU:1 before, /device:TPU:56 now
where the time goes in v1:
time: 156 us; the launch traced here: 155 us
  Pallas kernels  90 us (58%)
  blocking collectives  33 us (21%)
  starting transfers between devices  24.5 us (16%)
  waiting for transfers between devices  5.09 us (3%)
    pallas_call x1, Pallas kernels, per_device(): pl.pallas_call(main_kernel, out_shape=jax.ShapeDtypeStruct((2 * GROUP, 8,...  86.4 us
    psum x2, blocking collectives, per_device(): kin = lax.psum(lax.psum(kin, 'yhi'), 'bead')  33 us
    all_to_all x1, starting transfers between devices, per_device(): lax.all_to_all(packed, ('grp', 'mem'), split_axis=0, concat_axis=0, tiled...  10.6 us
    ppermute x1, starting transfers between devices, per_device(): after = lax.ppermute(offsets[:, :1], 'bead', [(j, i) for i, j in up])  4.55 us
    ppermute x1, waiting for transfers between devices, per_device(): far = lax.ppermute(ends, ('yhi', 'grp', 'mem'), swap)  4.33 us
    ppermute x1, starting transfers between devices, per_device(): before = lax.ppermute(offsets[:, 3:], 'bead', up)  3.4 us
    all_to_all x1, starting transfers between devices, per_device(): lax.all_to_all(done.reshape(GROUP, 2, 8, BLOCK), 'mem', split_axis=0, con...  3.27 us
  transfers between devices with their start and end apart: 5, of which 2 were waited for; matrix products, arithmetic and copies ran while one was open for 0% of the time, Pallas kernels for 56%

profile of v1, /device:TPU:56, one launch (start us, length us, event | category | flops | bytes accessed | tf_op | source)
XLA Modules:
  0.0 155.1 jit_solution(3873432596217186241)
XLA Ops:
  0.6 1.6 %pack.1 = f32[16,8,256]{2,1,0:T(8,128)} custom-call(s32[1]{0:T(128)} %bitcast.slab_ref, s32[2,4]{1,0:T(2,128)} %tiles_ref.1, f32[3,256]{1,0:T(4,128)} %cen_ref.1, f32[3,4,256]{2,1,0:T(4,128)} %off_ref.3, f32[3,4,256]{2,1,0:T(4,128)} %vel_ref.3, f32[1,256]{1,0:T(1,128)} %bitcast.11, f32[1,256]{1,0:T(1,128)} %bitcast.12, f32[1,256]{1,0:T(1,128)} %bitcast.9, ...), custom_call_target="tpu_custom_call" | custom-call | tf_op jit(solution)/shard_map/pack/pallas_call | solution.py:315
  2.2 0.0 copy-start.1
  2.2 10.6 %all-to-all-start = ((f32[16,8,256]{2,1,0:T(8,128)}), f32[16,8,256]{2,1,0:T(8,128)S(1)}, u32[]{:S(2)}, u32[]{:S(2)}) async-start(f32[16,8,256]{2,1,0:T(8,128)} %pack.1), calls=%async_computation | async-start | bytes 262144 | tf_op jit(solution)/shard_map/all_to_all | solution.py:322
  12.8 0.0 copy-done.1
  12.8 3.4 %collective-permute-start.1 = (f32[3,1,256]{2,1,0:T(1,128)S(1)}, f32[3,1,256]{2,1,0:T(1,128)S(1)}, u32[]{:S(2)}, u32[]{:S(2)}) collective-permute-start(f32[3,1,256]{2,1,0:T(1,128)S(1)} %get-tuple-element.5), channel_id=1, source_target_pairs={{0,1},{1,2},{2,3},{3,4},{4,5},{5,6},{6,7},{7,0},{8,9},{9,10},{10,1... | collective-permute-start | bytes 9224 | tf_op jit(solution)/shard_map/ppermute | solution.py:334
  16.2 4.6 %collective-permute-start.2 = (f32[3,1,256]{2,1,0:T(1,128)S(1)}, f32[3,1,256]{2,1,0:T(1,128)S(1)}, u32[]{:S(2)}, u32[]{:S(2)}) collective-permute-start(f32[3,1,256]{2,1,0:T(1,128)S(1)} %get-tuple-element.4), channel_id=1, source_target_pairs={{1,0},{2,1},{3,2},{4,3},{5,4},{6,5},{7,6},{0,7},{9,8},{10,9},{11,1... | collective-permute-start | bytes 9224 | tf_op jit(solution)/shard_map/ppermute | solution.py:335
  20.8 0.7 all-to-all-done.v_ref
  21.5 2.7 %collective-permute-start = (f32[5,8,256]{2,1,0:T(8,128)S(1)}, f32[5,8,256]{2,1,0:T(8,128)S(1)}, u32[]{:S(2)}, u32[]{:S(2)}) collective-permute-start(f32[5,8,256]{2,1,0:T(8,128)S(1)} %constant_dynamic-slice_fusion), channel_id=1, source_target_pairs={{0,128},{8,136},{16,144},{24,152},{32,160},{40,168},{48,176},{56,1... | collective-permute-start | bytes 122888 | tf_op jit(solution)/shard_map/ppermute | solution.py:329
  24.2 0.1 pad_add_fusion.place_ref
  24.3 4.3 %collective-permute-done.h_ref = f32[5,8,256]{2,1,0:T(8,128)S(1)} collective-permute-done((f32[5,8,256]{2,1,0:T(8,128)S(1)}, f32[5,8,256]{2,1,0:T(8,128)S(1)}, u32[]{:S(2)}, u32[]{:S(2)}) %collective-permute-start) | collective-permute-done | bytes 40992 | tf_op jit(solution)/shard_map/ppermute | solution.py:329
  28.6 86.4 %dipoles.1 = f32[8,8,128]{2,1,0:T(8,128)} custom-call(s32[2]{0:T(128)S(1)} %pad_add_fusion.place_ref, f32[16,8,256]{2,1,0:T(8,128)S(1)} %all-to-all-done.v_ref, f32[5,8,256]{2,1,0:T(8,128)S(1)} %collective-permute-done.h_ref), custom_call_target="tpu_custom_call" | custom-call | flops 400000000 | bytes 300000 | tf_op jit(solution)/shard_map/dipoles/pallas_call | solution.py:338
  115.0 3.3 %all-to-all-start.1 = ((f32[4,2,8,128]{3,2,1,0:T(8,128)}), f32[4,2,8,128]{3,2,1,0:T(8,128)S(1)}, u32[]{:S(2)}, u32[]{:S(2)}) async-start(f32[4,2,8,128]{3,2,1,0:T(8,128)} %bitcast.8), calls=%async_computation.1 | async-start | bytes 65536 | tf_op jit(solution)/shard_map/all_to_all | solution.py:361
  118.3 0.6 slice_reduce_fusion
  118.9 12.6 %psum.14 = f32[]{:T(128)} all-reduce(f32[]{:T(128)} %slice_reduce_fusion), channel_id=1, replica_groups=mesh['yhi'=4,'grp'=4,'mem'=4,'bead'=8] {'yhi'}, use_global_device_ids=true, to_apply=%region_1.2 | all-reduce | flops 1 | bytes 8 | tf_op jit(solution)/shard_map/psum | solution.py:332
  131.5 20.4 %psum.15.kin_ref = f32[1,1]{1,0:T(1,128)} all-reduce(f32[1,1]{1,0:T(1,128)} %bitcast.5), channel_id=1, replica_groups=mesh['yhi'=4,'grp'=4,'mem'=4,'bead'=8] {'bead'}, use_global_device_ids=true, to_apply=%region_2.3 | all-reduce | flops 1 | bytes 8 | tf_op jit(solution)/shard_map/psum | solution.py:332
  151.9 0.0 collective-permute-done.1.before_ref
  151.9 0.0 copy-start.2
  151.9 0.0 collective-permute-done.2.after_ref
  151.9 0.0 copy-start.3
  151.9 0.0 all-to-all-done.1.r_ref
  151.9 0.6 copy-done.2
  152.5 0.0 copy-done.3
  152.5 0.6 copy-done
  153.1 2.0 %finish.1 = (f32[3,4,256]{2,1,0:T(4,128)}, f32[3,4,256]{2,1,0:T(4,128)}, f32[3,4,256]{2,1,0:T(4,128)}, f32[3,4,256]{2,1,0:T(4,128)}) custom-call(f32[1,1]{1,0:T(1,128)} %psum.15.kin_ref, f32[4,2,8,128]{3,2,1,0:T(8,128)} %copy-done, f32[3,4,256]{2,1,0:T(4,128)} %off_ref.3, f32[3,1,256]{2,1,0:T(1,128)} %copy-done.2, f32[3,1,256]{2,1,0:T(1,128)} %copy-done.3, ...), custom_call_target="tpu_custom_call" | custom-call | tf_op jit(solution)/shard_map/finish/pallas_call | solution.py:363
  (3 shorter events, 0.0 us)
Async XLA Ops:
  2.2 10.6 %copy-start.1 = (f32[3,4,256]{2,1,0:T(4,128)S(1)}, f32[3,4,256]{2,1,0:T(4,128)}, u32[]{:S(2)}) copy-start(f32[3,4,256]{2,1,0:T(4,128)} %off_ref.3) | copy-start | bytes 36868
  2.2 19.3 %all-to-all-start = ((f32[16,8,256]{2,1,0:T(8,128)}), f32[16,8,256]{2,1,0:T(8,128)S(1)}, u32[]{:S(2)}, u32[]{:S(2)}) async-start(f32[16,8,256]{2,1,0:T(8,128)} %pack.1), calls=%async_computation | async-start | bytes 262144 | tf_op jit(solution)/shard_map/all_to_all | solution.py:322
  12.8 139.1 %collective-permute-start.1 = (f32[3,1,256]{2,1,0:T(1,128)S(1)}, f32[3,1,256]{2,1,0:T(1,128)S(1)}, u32[]{:S(2)}, u32[]{:S(2)}) collective-permute-start(f32[3,1,256]{2,1,0:T(1,128)S(1)} %get-tuple-element.5), channel_id=1, source_target_pairs={{0,1},{1,2},{2,3},{3,4},{4,5},{5,6},{6,7},{7,0},{8,9},{9,10},{10,1... | collective-permute-start | bytes 9224 | tf_op jit(solution)/shard_map/ppermute | solution.py:334
  16.2 135.7 %collective-permute-start.2 = (f32[3,1,256]{2,1,0:T(1,128)S(1)}, f32[3,1,256]{2,1,0:T(1,128)S(1)}, u32[]{:S(2)}, u32[]{:S(2)}) collective-permute-start(f32[3,1,256]{2,1,0:T(1,128)S(1)} %get-tuple-element.4), channel_id=1, source_target_pairs={{1,0},{2,1},{3,2},{4,3},{5,4},{6,5},{7,6},{0,7},{9,8},{10,9},{11,1... | collective-permute-start | bytes 9224 | tf_op jit(solution)/shard_map/ppermute | solution.py:335
  21.5 7.1 %collective-permute-start = (f32[5,8,256]{2,1,0:T(8,128)S(1)}, f32[5,8,256]{2,1,0:T(8,128)S(1)}, u32[]{:S(2)}, u32[]{:S(2)}) collective-permute-start(f32[5,8,256]{2,1,0:T(8,128)S(1)} %constant_dynamic-slice_fusion), channel_id=1, source_target_pairs={{0,128},{8,136},{16,144},{24,152},{32,160},{40,168},{48,176},{56,1... | collective-permute-start | bytes 122888 | tf_op jit(solution)/shard_map/ppermute | solution.py:329
  115.0 36.9 %all-to-all-start.1 = ((f32[4,2,8,128]{3,2,1,0:T(8,128)}), f32[4,2,8,128]{3,2,1,0:T(8,128)S(1)}, u32[]{:S(2)}, u32[]{:S(2)}) async-start(f32[4,2,8,128]{3,2,1,0:T(8,128)} %bitcast.8), calls=%async_computation.1 | async-start | bytes 65536 | tf_op jit(solution)/shard_map/all_to_all | solution.py:361
  151.9 0.6 copy-start.2
  151.9 0.6 copy-start.3
  152.5 0.6 copy-start

commit v2 on v1

--- a/solution.py
+++ b/solution.py
@@ -35,8 +35,8 @@
 SMEM = pl.BlockSpec(memory_space=pltpu.SMEM)
 
 
-def pack_kernel(slab_ref, tiles_ref, cen_ref, off_ref, vel_ref, q_ref, a_ref, m_ref, g_ref, out_ref):
-    slab = slab_ref[0].astype(F32)
+def pack_kernel(place_ref, tiles_ref, cen_ref, off_ref, vel_ref, q_ref, a_ref, m_ref, g_ref, out_ref):
+    slab = place_ref[3].astype(F32)
     bx = (slab + cen_ref[0:1, :]) * slab_width
     by = cen_ref[1:2, :] * box_side
     bz = cen_ref[2:3, :] * box_side
@@ -71,17 +71,7 @@
 
 
 def rows_of(acc):
-    ones = jnp.ones((8, BLOCK), F32)
-    return lax.dot_general(
-        ones, acc, (((1,), (1,)), ((), ())), precision=lax.Precision.HIGHEST, preferred_element_type=F32
-    )
-
-
-def distances(ci, cj, kf, ki):
-    dx = column(kf, 0) - ci[0]
-    dy = (ki[0] - cj[0]).astype(F32) * (1.0 / STEPS)
-    dz = (ki[1] - cj[1]).astype(F32) * (1.0 / STEPS)
-    return dx, dy, dz
+    return jnp.broadcast_to(jnp.sum(jnp.transpose(acc), axis=0, keepdims=True), (8, BLOCK))
 
 
 def main_kernel(
@@ -116,7 +106,7 @@
             coli[pl.ds(at, BLOCK), :] = jnp.transpose(fixed)
         return carry
 
-    lax.fori_loop(0, WINDOW, load_slab, 0)
+    lax.fori_loop(0, WINDOW, load_slab, 0, unroll=7)
     copy = pltpu.make_async_copy(marks_v, marks, sem)
     copy.start()
     copy.wait()
@@ -129,7 +119,19 @@
         at = pl.multiple_of(blk * BLOCK + i * 8, 8)
         return colf[pl.ds(at, 8), :], coli[pl.ds(at, 8), :]
 
-    def field_block(blk, carry):
+    def pipelined(start, stop, pairs, rows):
+        def two(n, carry):
+            blk = start + 2 * n
+            pairs(blk, 0)
+            rows(blk - 1, 1)
+            pairs(blk + 1, 1)
+            rows(blk, 0)
+            return carry
+
+        lax.fori_loop(0, (stop - start) // 2, two, 0)
+        rows(stop - 1, 1)
+
+    def field_block(blk, half):
         src = [source(blk, k) for k in range(NT)]
         slot = jnp.where(jnp.logical_and(blk >= 4, blk < WBLK - 4), blk - 4, KEPT)
 
@@ -161,19 +163,20 @@
                 w = b3 * srcf[s, 1]
                 sums = [sums[0] + w * dx, sums[1] + w * dy, sums[2] + w * dz]
             for n in range(3):
-                acc[n, pl.ds(at, 8), :] = sums[n]
+                acc[half, n, pl.ds(at, 8), :] = sums[n]
             return carry
 
-        lax.fori_loop(0, 16, tile, 0, unroll=2)
+        lax.fori_loop(0, 16, tile, 0, unroll=16)
+
+    def field_rows(blk, half):
         for n in range(3):
-            rows = rows_of(acc[n])
+            rows = rows_of(acc[half, n])
             field[blk, n] = rows
             mu_a[blk, n] = srcf[blk, 4] * rows
-        return carry
-
-    lax.fori_loop(2, WBLK - 2, field_block, 0)
-
-    def mutual_block(old, new, blk, carry):
+
+    pipelined(2, WBLK - 2, field_block, field_rows)
+
+    def mutual_block(old, blk, half):
         src = [source(blk, k) for k in range(NT)]
         mus = [[old[src[k], n] for n in range(3)] for k in range(NT)]
 
@@ -190,18 +193,19 @@
                     sums[2] + (w * dz - b3 * mz),
                 ]
             for n in range(3):
-                acc[n, pl.ds(at, 8), :] = sums[n]
+                acc[half, n, pl.ds(at, 8), :] = sums[n]
             return carry
 
-        lax.fori_loop(0, 16, tile, 0, unroll=4)
+        lax.fori_loop(0, 16, tile, 0, unroll=16)
+
+    def mutual_rows(new, blk, half):
         for n in range(3):
-            new[blk, n] = srcf[blk, 4] * (field[blk, n] + rows_of(acc[n]))
-        return carry
+            new[blk, n] = srcf[blk, 4] * (field[blk, n] + rows_of(acc[half, n]))
 
     old, new = mu_a, mu_b
     for step in range(ITERS):
         edge = 4 + 2 * step
-        lax.fori_loop(edge, WBLK - edge, functools.partial(mutual_block, old, new), 0)
+        pipelined(edge, WBLK - edge, functools.partial(mutual_block, old), functools.partial(mutual_rows, new))
         old, new = new, old
     mu = old
 
@@ -225,12 +229,12 @@
             c_of.append(0.5 * (here + there))
         own = [mu[blk, n] * (1.0 / UNIT) for n in range(3)]
         col = jnp.where(line == 0, own[0], jnp.where(line == 1, own[1], own[2]))
-        acc[3, :, 0:8] = jnp.transpose(col)
+        acc[0, 3, :, 0:8] = jnp.transpose(col)
 
         def tile(i, carry):
             kf, ki = targets(i, blk)
             at = pl.multiple_of(i * 8, 8)
-            km = acc[3, pl.ds(at, 8), 0:8]
+            km = acc[0, 3, pl.ds(at, 8), 0:8]
             xi, gi, idi, qi = column(kf, 0), column(kf, 7), column(kf, 5), column(kf, 3)
             yi, zi = column(ki, 1), column(ki, 2)
             ax, ay, az = column(km, 0), column(km, 1), column(km, 2)
@@ -270,30 +274,44 @@
                 fx = fx + (g * bx + k2 * dx)
                 fy = fy + (g * by + k2 * dy)
                 fz = fz + (g * bz + k2 * dz)
-            acc[0, pl.ds(at, 8), :] = fx + along * ax
-            acc[1, pl.ds(at, 8), :] = fy + along * ay
-            acc[2, pl.ds(at, 8), :] = fz + along * az
+            acc[0, 0, pl.ds(at, 8), :] = fx + along * ax
+            acc[0, 1, pl.ds(at, 8), :] = fy + along * ay
+            acc[0, 2, pl.ds(at, 8), :] = fz + along * az
             return carry
 
-        lax.fori_loop(0, 16, tile, 0, unroll=2)
+        lax.fori_loop(0, 16, tile, 0, unroll=16)
         res = jnp.zeros((8, BLOCK), F32)
         for n in range(3):
             res = jnp.where(line == n, own[n], res)
-            res = jnp.where(line == n + 3, rows_of(acc[n]), res)
+            res = jnp.where(line == n + 3, rows_of(acc[0, n]), res)
         out_ref[n_own] = res
         return carry
 
     lax.fori_loop(0, 2 * GROUP, force_block, 0)
 
 
-def final_kernel(kin_ref, r_ref, off_ref, before_ref, after_ref, vel_ref, m_ref, mu_ref, f_ref, nv_ref, no_ref):
-    kinetic = kin_ref[...] * (1.0 / 1572864.0)
+def middle_kernel(place_ref, got_ref, off_ref, ends_ref, msg_ref):
+    start = jnp.where(place_ref[0] < 2, ROW - HALO, 0)
+    for n in range(HALO):
+        ends_ref[n] = got_ref[start + n]
+    kin = jnp.sum(got_ref[...], axis=0)[7:8]
+    last = [off_ref[n, 3:4, :] for n in range(3)]
+    first = [off_ref[n, 0:1, :] for n in range(3)]
+    msg = jnp.concatenate(last + first + [kin, kin], axis=0)
+    msg_ref[...] = jnp.broadcast_to(msg[None], msg_ref.shape)
+
+
+def final_kernel(place_ref, r_ref, msg_ref, off_ref, vel_ref, m_ref, mu_ref, f_ref, nv_ref, no_ref):
+    kinetic = jnp.sum(msg_ref[...], axis=0)[7:8] * (1.0 / 1572864.0)
     scale = jnp.sqrt(1.0 + coupling * (target_temp / kinetic - 1.0))
     inv = 1.0 / m_ref[...]
+    bead = place_ref[2]
+    left = msg_ref[place_ref[1] * 8 + lax.rem(bead + 7, 8)]
+    right = msg_ref[place_ref[1] * 8 + lax.rem(bead + 1, 8)]
     for n in range(3):
         off = off_ref[n]
-        before = jnp.concatenate([before_ref[n], off[:3]], axis=0)
-        after = jnp.concatenate([off[1:], after_ref[n]], axis=0)
+        before = jnp.concatenate([left[n : n + 1], off[:3]], axis=0)
+        after = jnp.concatenate([off[1:], right[n + 3 : n + 4]], axis=0)
         restoring = -bond_coef * (2.0 * off - before - after)
         mu = jnp.concatenate(
             [jnp.concatenate([r_ref[r, b, n : n + 1, :] for b in range(2)], axis=1) for r in range(4)], axis=0
@@ -308,34 +326,8 @@
         no_ref[n] = off + time_step * nv
 
 
-def per_device(centroids, offsets, velocities, charges, polar, masses, groups, tiles):
-    yhi, grp, mem = lax.axis_index("yhi"), lax.axis_index("grp"), lax.axis_index("mem")
-    slab = ((yhi * 4 + grp) * 4 + mem).astype(I32)
-    line = lambda a: a.reshape(1, 256)
-    packed = pl.pallas_call(
-        pack_kernel,
-        out_shape=jax.ShapeDtypeStruct((ROW, 8, 256), F32),
-        in_specs=[SMEM, SMEM] + [VMEM] * 7,
-        out_specs=VMEM,
-        name="pack",
-    )(slab.reshape(1), tiles, centroids, offsets, velocities, line(charges), line(polar), line(masses), line(groups))
-    got = lax.all_to_all(packed, ("grp", "mem"), split_axis=0, concat_axis=0, tiled=True)
-    swap = []
-    for y in range(4):
-        for i in range(ROW):
-            to = (y + (1 if i < ROW // 2 else -1)) % 4
-            swap.append((y * ROW + i, to * ROW + i))
-    ends = lax.dynamic_slice_in_dim(got, jnp.where(grp < 2, ROW - HALO, 0), HALO, axis=0)
-    far = lax.ppermute(ends, ("yhi", "grp", "mem"), swap)
-
-    kin = jnp.sum(got[:, 7, 0])
-    kin = lax.psum(lax.psum(kin, "yhi"), "bead")
-    up = [(i, (i + 1) % 8) for i in range(8)]
-    before = lax.ppermute(offsets[:, 3:], "bead", up)
-    after = lax.ppermute(offsets[:, :1], "bead", [(j, i) for i, j in up])
-
-    place = jnp.stack([grp, yhi]).astype(I32)
-    done = pl.pallas_call(
+def call_main(place, got, far):
+    return pl.pallas_call(
         main_kernel,
         out_shape=jax.ShapeDtypeStruct((2 * GROUP, 8, BLOCK), F32),
         in_specs=[SMEM, VMEM, VMEM],
@@ -348,7 +340,7 @@
             pltpu.VMEM((16, BLOCK), I32),
             pltpu.SMEM((16, BLOCK), I32),
             pltpu.VMEM((KEPT + 1, NT, 5, BLOCK, BLOCK), F32),
-            pltpu.VMEM((4, BLOCK, BLOCK), F32),
+            pltpu.VMEM((2, 4, BLOCK, BLOCK), F32),
             pltpu.VMEM((WBLK, 3, 8, BLOCK), F32),
             pltpu.VMEM((WBLK, 3, 8, BLOCK), F32),
             pltpu.VMEM((WBLK, 3, 8, BLOCK), F32),
@@ -358,15 +350,48 @@
         cost_estimate=pl.CostEstimate(flops=400_000_000, bytes_accessed=300_000, transcendentals=0),
         name="dipoles",
     )(place, got, far)
+
+
+def per_device(centroids, offsets, velocities, charges, polar, masses, groups, tiles):
+    yhi, grp, mem, bead = [lax.axis_index(a) for a in ("yhi", "grp", "mem", "bead")]
+    slab = ((yhi * 4 + grp) * 4 + mem).astype(I32)
+    place = jnp.stack([grp, yhi, bead, slab]).astype(I32)
+    line = lambda a: a.reshape(1, 256)
+    small = pltpu.CompilerParams(vmem_limit_bytes=4 * 2**20)
+    packed = pl.pallas_call(
+        pack_kernel,
+        out_shape=jax.ShapeDtypeStruct((ROW, 8, 256), F32),
+        in_specs=[SMEM, SMEM] + [VMEM] * 7,
+        out_specs=VMEM,
+        name="pack",
+    )(place, tiles, centroids, offsets, velocities, line(charges), line(polar), line(masses), line(groups))
+    got = lax.all_to_all(packed, ("grp", "mem"), split_axis=0, concat_axis=0, tiled=True)
+    ends, msg = pl.pallas_call(
+        middle_kernel,
+        out_shape=(jax.ShapeDtypeStruct((HALO, 8, 256), F32), jax.ShapeDtypeStruct((32, 8, 256), F32)),
+        in_specs=[SMEM, VMEM, VMEM],
+        out_specs=(VMEM, VMEM),
+        name="middle",
+    )(place, got, offsets)
+    swap = []
+    for y in range(4):
+        for i in range(ROW):
+            to = (y + (1 if i < ROW // 2 else -1)) % 4
+            swap.append((y * ROW + i, to * ROW + i))
+    far = lax.ppermute(ends, ("yhi", "grp", "mem"), swap)
+    msg = lax.all_to_all(msg, ("yhi", "bead"), split_axis=0, concat_axis=0, tiled=True)
+    done = call_main(place, got, far)
+    done, msg = lax.optimization_barrier((done, msg))
     back = lax.all_to_all(done.reshape(GROUP, 2, 8, BLOCK), "mem", split_axis=0, concat_axis=0, tiled=True)
     shape = jax.ShapeDtypeStruct((3, 4, 256), F32)
     return pl.pallas_call(
         final_kernel,
         out_shape=(shape,) * 4,
-        in_specs=[VMEM] * 7,
+        in_specs=[SMEM] + [VMEM] * 5,
         out_specs=(VMEM,) * 4,
+        compiler_params=small,
         name="finish",
-    )(kin.reshape(1, 1), back, offsets, before, after, velocities, line(masses))
+    )(place, back, msg, offsets, velocities, line(masses))
 
 
 def solution(mesh):

time: 156 us -> 94.4 us (0.61)
  the two profiles are of different devices: /device:TPU:56 before, /device:TPU:1 now
where the time goes in v2:
time: 94.4 us; the launch traced here: 94 us
  Pallas kernels  43.7 us (46%)
  blocking collectives  27.7 us (29%)
  starting transfers between devices  13.8 us (15%)
  waiting for transfers between devices  7.36 us (8%)
    pallas_call x1, Pallas kernels, call_main(): pl.pallas_call(main_kernel, out_shape=jax.ShapeDtypeStruct((2 * GROUP, 8,...  39.3 us
    all_to_all x1, blocking collectives, per_device(): lax.all_to_all(packed, ('grp', 'mem'), split_axis=0, concat_axis=0, tiled...  21.1 us
    all_to_all x1, starting transfers between devices, per_device(): lax.all_to_all(msg, ('yhi', 'bead'), split_axis=0, concat_axis=0, tiled=T...  9.8 us
    ppermute x1, waiting for transfers between devices, per_device(): far = lax.ppermute(ends, ('yhi', 'grp', 'mem'), swap)  7.36 us
    all_to_all x1, blocking collectives, per_device(): lax.all_to_all(done.reshape(GROUP, 2, 8, BLOCK), 'mem', split_axis=0, con...  6.58 us
    ppermute x1, starting transfers between devices, per_device(): far = lax.ppermute(ends, ('yhi', 'grp', 'mem'), swap)  4.04 us
  transfers between devices with their start and end apart: 2, of which 1 were waited for; matrix products, arithmetic and copies ran while one was open for 0% of the time, Pallas kernels for 42%

profile of v2, /device:TPU:1, one launch (start us, length us, event | category | flops | bytes accessed | tf_op | source)
XLA Modules:
  0.0 94.0 jit_solution(8445063926880466358)
XLA Ops:
  0.6 0.7 pad_add_fusion.place_ref
  1.3 1.6 %pack.1 = f32[16,8,256]{2,1,0:T(8,128)} custom-call(s32[4]{0:T(128)} %pad_add_fusion.place_ref, s32[2,4]{1,0:T(2,128)} %tiles_ref.1, f32[3,256]{1,0:T(4,128)} %cen_ref.1, f32[3,4,256]{2,1,0:T(4,128)} %off_ref.5, f32[3,4,256]{2,1,0:T(4,128)} %vel_ref.3, f32[1,256]{1,0:T(1,128)} %bitcast.12, f32[1,256]{1,0:T(1,128)} %bitcast.13, f32[1,256]{1,0:T(1,128)} %bitcast.10, ...), custom_call_target="tpu_custom_call" | custom-call | tf_op jit(solution)/shard_map/pack/pallas_call | solution.py:361
  2.9 21.1 %all_to_all.15.got_ref.v_ref = f32[16,8,256]{2,1,0:T(8,128)} all-to-all(f32[16,8,256]{2,1,0:T(8,128)} %pack.1), channel_id=1, replica_groups=mesh['yhi'=4,'grp'=4,'mem'=4,'bead'=8] {'grp','mem'}, dimensions={0} | all-to-all | bytes 262144 | tf_op jit(solution)/shard_map/all_to_all | solution.py:368
  24.0 1.6 %middle.1 = (f32[5,8,256]{2,1,0:T(8,128)}, f32[32,8,256]{2,1,0:T(8,128)}) custom-call(s32[4]{0:T(128)} %pad_add_fusion.place_ref, f32[16,8,256]{2,1,0:T(8,128)} %all_to_all.15.got_ref.v_ref, f32[3,4,256]{2,1,0:T(4,128)} %off_ref.5), custom_call_target="tpu_custom_call" | custom-call | tf_op jit(solution)/shard_map/middle/pallas_call | solution.py:369
  25.6 0.0 copy-start.5
  25.6 0.0 copy-start
  25.6 9.8 %all-to-all-start.1 = ((f32[32,8,256]{2,1,0:T(8,128)}), f32[32,8,256]{2,1,0:T(8,128)S(1)}, u32[]{:S(2)}, u32[]{:S(2)}) async-start(f32[32,8,256]{2,1,0:T(8,128)} %get-tuple-element.9), calls=%async_computation.1 | async-start | bytes 524288 | tf_op jit(solution)/shard_map/all_to_all | solution.py:382
  35.4 0.0 copy-start.3
  35.5 0.0 copy-done.5
  35.5 4.0 %collective-permute-start = (f32[5,8,256]{2,1,0:T(8,128)S(1)}, f32[5,8,256]{2,1,0:T(8,128)S(1)}, u32[]{:S(2)}, u32[]{:S(2)}) collective-permute-start(f32[5,8,256]{2,1,0:T(8,128)S(1)} %copy-done.5), channel_id=1, source_target_pairs={{0,128},{8,136},{16,144},{24,152},{32,160},{40,168},{48,176},{56,1... | collective-permute-start | bytes 122888 | tf_op jit(solution)/shard_map/ppermute | solution.py:381
  39.5 7.4 %collective-permute-done.h_ref = f32[5,8,256]{2,1,0:T(8,128)S(1)} collective-permute-done((f32[5,8,256]{2,1,0:T(8,128)S(1)}, f32[5,8,256]{2,1,0:T(8,128)S(1)}, u32[]{:S(2)}, u32[]{:S(2)}) %collective-permute-start) | collective-permute-done | bytes 40992 | tf_op jit(solution)/shard_map/ppermute | solution.py:381
  46.9 0.0 copy-done
  46.9 0.0 copy-done.3
  46.9 39.3 %dipoles.1 = f32[8,8,128]{2,1,0:T(8,128)S(1)} custom-call(s32[4]{0:T(128)S(1)} %copy-done.3, f32[16,8,256]{2,1,0:T(8,128)S(1)} %copy-done, f32[5,8,256]{2,1,0:T(8,128)S(1)} %collective-permute-done.h_ref), custom_call_target="tpu_custom_call" | custom-call | flops 400000000 | bytes 300000 | tf_op jit(solution)/shard_map/dipoles/pallas_call | solution.py:330
  86.1 0.0 all-to-all-done.1.msg_ref
  86.2 0.0 copy-start.1
  86.2 0.0 copy-start.2
  86.2 0.0 copy-start.4
  86.2 6.6 %all_to_all.16.r_ref = f32[4,2,8,128]{3,2,1,0:T(8,128)S(1)} all-to-all(f32[4,2,8,128]{3,2,1,0:T(8,128)S(1)} %bitcast.9), channel_id=1, replica_groups=mesh['yhi'=4,'grp'=4,'mem'=4,'bead'=8] {'mem'}, dimensions={0} | all-to-all | bytes 65536 | tf_op jit(solution)/shard_map/all_to_all | solution.py:385
  92.8 0.0 copy-done.1
  92.8 0.0 copy-done.2
  92.8 0.0 copy-done.4
  92.8 1.2 %finish.1 = (f32[3,4,256]{2,1,0:T(4,128)}, f32[3,4,256]{2,1,0:T(4,128)}, f32[3,4,256]{2,1,0:T(4,128)}, f32[3,4,256]{2,1,0:T(4,128)}) custom-call(s32[4]{0:T(128)S(1)} %copy-done.3, f32[4,2,8,128]{3,2,1,0:T(8,128)S(1)} %all_to_all.16.r_ref, f32[32,8,256]{2,1,0:T(8,128)S(1)} %all-to-all-done.1.msg_ref, f32[3,4,256]{2,1,0:T(4,128)S(1)} %copy-done.1, ...), custom_call_target="tpu_custom_call" | custom-call | tf_op jit(solution)/shard_map/finish/pallas_call | solution.py:387
Async XLA Ops:
  25.6 9.8 %copy-start.5 = (f32[5,8,256]{2,1,0:T(8,128)S(1)}, f32[5,8,256]{2,1,0:T(8,128)}, u32[]{:S(2)}) copy-start(f32[5,8,256]{2,1,0:T(8,128)} %get-tuple-element.8) | copy-start | bytes 122884
  25.6 21.2 %copy-start = (f32[16,8,256]{2,1,0:T(8,128)S(1)}, f32[16,8,256]{2,1,0:T(8,128)}, u32[]{:S(2)}) copy-start(f32[16,8,256]{2,1,0:T(8,128)} %all_to_all.15.got_ref.v_ref) | copy-start | bytes 393220
  25.6 60.5 %all-to-all-start.1 = ((f32[32,8,256]{2,1,0:T(8,128)}), f32[32,8,256]{2,1,0:T(8,128)S(1)}, u32[]{:S(2)}, u32[]{:S(2)}) async-start(f32[32,8,256]{2,1,0:T(8,128)} %get-tuple-element.9), calls=%async_computation.1 | async-start | bytes 524288 | tf_op jit(solution)/shard_map/all_to_all | solution.py:382
  35.4 11.4 %copy-start.3 = (s32[4]{0:T(128)S(1)}, s32[4]{0:T(128)}, u32[]{:S(2)}) copy-start(s32[4]{0:T(128)} %pad_add_fusion.place_ref) | copy-start | bytes 52
  35.5 11.4 %collective-permute-start = (f32[5,8,256]{2,1,0:T(8,128)S(1)}, f32[5,8,256]{2,1,0:T(8,128)S(1)}, u32[]{:S(2)}, u32[]{:S(2)}) collective-permute-start(f32[5,8,256]{2,1,0:T(8,128)S(1)} %copy-done.5), channel_id=1, source_target_pairs={{0,128},{8,136},{16,144},{24,152},{32,160},{40,168},{48,176},{56,1... | collective-permute-start | bytes 122888 | tf_op jit(solution)/shard_map/ppermute | solution.py:381
  86.2 6.6 %copy-start.1 = (f32[3,4,256]{2,1,0:T(4,128)S(1)}, f32[3,4,256]{2,1,0:T(4,128)}, u32[]{:S(2)}) copy-start(f32[3,4,256]{2,1,0:T(4,128)} %off_ref.5) | copy-start | bytes 36868
  86.2 6.6 %copy-start.2 = (f32[3,4,256]{2,1,0:T(4,128)S(1)}, f32[3,4,256]{2,1,0:T(4,128)}, u32[]{:S(2)}) copy-start(f32[3,4,256]{2,1,0:T(4,128)} %vel_ref.3) | copy-start | bytes 36868
  86.2 6.6 %copy-start.4 = (f32[256]{0:T(256)S(1)}, f32[256]{0:T(256)}, u32[]{:S(2)}) copy-start(f32[256]{0:T(256)} %param.13) | copy-start | bytes 3076

commit v3 on v2

--- a/solution.py
+++ b/solution.py
@@ -35,8 +35,8 @@
 SMEM = pl.BlockSpec(memory_space=pltpu.SMEM)
 
 
-def pack_kernel(place_ref, tiles_ref, cen_ref, off_ref, vel_ref, q_ref, a_ref, m_ref, g_ref, out_ref):
-    slab = place_ref[3].astype(F32)
+def pack_kernel(tiles_ref, cen_ref, off_ref, vel_ref, q_ref, a_ref, m_ref, g_ref, out_ref):
+    slab = ((lax.axis_index("yhi") * 4 + lax.axis_index("grp")) * 4 + lax.axis_index("mem")).astype(F32)
     bx = (slab + cen_ref[0:1, :]) * slab_width
     by = cen_ref[1:2, :] * box_side
     bz = cen_ref[2:3, :] * box_side
@@ -75,19 +75,20 @@
 
 
 def main_kernel(
-    place_ref, v_ref, h_ref, out_ref, srcf, srci, colf, coli, marks_v, marks, pair, acc, field, mu_a, mu_b, sem
+    v_ref, h_ref, out_ref, srcf, srci, colf, coli, marks_v, marks, pair, acc, field, mu_a, mu_b, sem
 ):
-    grp = place_ref[0]
-    row = place_ref[1]
+    grp = lax.axis_index("grp")
+    row = lax.axis_index("yhi")
     line = lax.broadcasted_iota(I32, (8, BLOCK), 0)
 
     def load_slab(w, carry):
         r = grp * GROUP - HALO + w
         inside = jnp.logical_and(r >= 0, r < ROW)
+        near = lax.rem(jnp.where(r < 0, row + 3, row + 1), 4)
         far = jnp.where(r < 0, r + HALO, r - ROW)
         slab = row * ROW + r
         shift = jnp.where(slab < 0, -576.0, jnp.where(slab >= 64, 576.0, 0.0)).astype(F32)
-        whole = jnp.where(inside, v_ref[jnp.clip(r, 0, ROW - 1)], h_ref[jnp.clip(far, 0, HALO - 1)])
+        whole = jnp.where(inside, v_ref[jnp.clip(r, 0, ROW - 1)], h_ref[near, jnp.clip(far, 0, HALO - 1)])
         marks_v[pl.ds(w, 1), :] = whole[6:7, :BLOCK].astype(I32)
         for half in range(2):
             blk = 2 * w + half
@@ -290,24 +291,31 @@
     lax.fori_loop(0, 2 * GROUP, force_block, 0)
 
 
-def middle_kernel(place_ref, got_ref, off_ref, ends_ref, msg_ref):
-    start = jnp.where(place_ref[0] < 2, ROW - HALO, 0)
-    for n in range(HALO):
-        ends_ref[n] = got_ref[start + n]
-    kin = jnp.sum(got_ref[...], axis=0)[7:8]
+def middle_kernel(got_ref, ends_ref):
+    row = lax.axis_index("yhi")
+    line = lax.broadcasted_iota(I32, (8, 256), 0)
+    kin = jnp.sum(got_ref[...], axis=0)
+    for d in range(4):
+        start = jnp.where(lax.rem(row + 3, 4) == d, 0, ROW - HALO)
+        for n in range(HALO):
+            ends_ref[d, n] = jnp.where(line == 7, kin, got_ref[start + n])
+
+
+def edges_kernel(far_ref, off_ref, msg_ref):
+    kin = jnp.sum(far_ref[:, 0], axis=0)[7:8]
     last = [off_ref[n, 3:4, :] for n in range(3)]
     first = [off_ref[n, 0:1, :] for n in range(3)]
     msg = jnp.concatenate(last + first + [kin, kin], axis=0)
     msg_ref[...] = jnp.broadcast_to(msg[None], msg_ref.shape)
 
 
-def final_kernel(place_ref, r_ref, msg_ref, off_ref, vel_ref, m_ref, mu_ref, f_ref, nv_ref, no_ref):
+def final_kernel(r_ref, msg_ref, off_ref, vel_ref, m_ref, mu_ref, f_ref, nv_ref, no_ref):
     kinetic = jnp.sum(msg_ref[...], axis=0)[7:8] * (1.0 / 1572864.0)
     scale = jnp.sqrt(1.0 + coupling * (target_temp / kinetic - 1.0))
     inv = 1.0 / m_ref[...]
-    bead = place_ref[2]
-    left = msg_ref[place_ref[1] * 8 + lax.rem(bead + 7, 8)]
-    right = msg_ref[place_ref[1] * 8 + lax.rem(bead + 1, 8)]
+    bead = lax.axis_index("bead")
+    left = msg_ref[lax.rem(bead + 7, 8)]
+    right = msg_ref[lax.rem(bead + 1, 8)]
     for n in range(3):
         off = off_ref[n]
         before = jnp.concatenate([left[n : n + 1], off[:3]], axis=0)
@@ -326,11 +334,11 @@
         no_ref[n] = off + time_step * nv
 
 
-def call_main(place, got, far):
+def call_main(got, far):
     return pl.pallas_call(
         main_kernel,
         out_shape=jax.ShapeDtypeStruct((2 * GROUP, 8, BLOCK), F32),
-        in_specs=[SMEM, VMEM, VMEM],
+        in_specs=[VMEM, VMEM],
         out_specs=VMEM,
         scratch_shapes=[
             pltpu.VMEM((WBLK, 5, 8, BLOCK), F32),
@@ -349,49 +357,49 @@
         compiler_params=pltpu.CompilerParams(vmem_limit_bytes=50 * 2**20),
         cost_estimate=pl.CostEstimate(flops=400_000_000, bytes_accessed=300_000, transcendentals=0),
         name="dipoles",
-    )(place, got, far)
+    )(got, far)
 
 
 def per_device(centroids, offsets, velocities, charges, polar, masses, groups, tiles):
-    yhi, grp, mem, bead = [lax.axis_index(a) for a in ("yhi", "grp", "mem", "bead")]
-    slab = ((yhi * 4 + grp) * 4 + mem).astype(I32)
-    place = jnp.stack([grp, yhi, bead, slab]).astype(I32)
     line = lambda a: a.reshape(1, 256)
     small = pltpu.CompilerParams(vmem_limit_bytes=4 * 2**20)
     packed = pl.pallas_call(
         pack_kernel,
         out_shape=jax.ShapeDtypeStruct((ROW, 8, 256), F32),
-        in_specs=[SMEM, SMEM] + [VMEM] * 7,
+        in_specs=[SMEM] + [VMEM] * 7,
         out_specs=VMEM,
         name="pack",
-    )(place, tiles, centroids, offsets, velocities, line(charges), line(polar), line(masses), line(groups))
+    )(tiles, centroids, offsets, velocities, line(charges), line(polar), line(masses), line(groups))
     got = lax.all_to_all(packed, ("grp", "mem"), split_axis=0, concat_axis=0, tiled=True)
-    ends, msg = pl.pallas_call(
+    ends = pl.pallas_call(
         middle_kernel,
-        out_shape=(jax.ShapeDtypeStruct((HALO, 8, 256), F32), jax.ShapeDtypeStruct((32, 8, 256), F32)),
-        in_specs=[SMEM, VMEM, VMEM],
-        out_specs=(VMEM, VMEM),
+        out_shape=jax.ShapeDtypeStruct((4, HALO, 8, 256), F32),
+        in_specs=[VMEM],
+        out_specs=VMEM,
+        compiler_params=small,
         name="middle",
-    )(place, got, offsets)
-    swap = []
-    for y in range(4):
-        for i in range(ROW):
-            to = (y + (1 if i < ROW // 2 else -1)) % 4
-            swap.append((y * ROW + i, to * ROW + i))
-    far = lax.ppermute(ends, ("yhi", "grp", "mem"), swap)
-    msg = lax.all_to_all(msg, ("yhi", "bead"), split_axis=0, concat_axis=0, tiled=True)
-    done = call_main(place, got, far)
+    )(got)
+    far = lax.all_to_all(ends, "yhi", split_axis=0, concat_axis=0, tiled=True)
+    msg = pl.pallas_call(
+        edges_kernel,
+        out_shape=jax.ShapeDtypeStruct((8, 8, 256), F32),
+        in_specs=[VMEM, VMEM],
+        out_specs=VMEM,
+        name="edges",
+    )(far, offsets)
+    msg = lax.all_to_all(msg, "bead", split_axis=0, concat_axis=0, tiled=True)
+    done = call_main(got, far)
     done, msg = lax.optimization_barrier((done, msg))
     back = lax.all_to_all(done.reshape(GROUP, 2, 8, BLOCK), "mem", split_axis=0, concat_axis=0, tiled=True)
     shape = jax.ShapeDtypeStruct((3, 4, 256), F32)
     return pl.pallas_call(
         final_kernel,
         out_shape=(shape,) * 4,
-        in_specs=[SMEM] + [VMEM] * 5,
+        in_specs=[VMEM] * 5,
         out_specs=(VMEM,) * 4,
         compiler_params=small,
         name="finish",
-    )(place, back, msg, offsets, velocities, line(masses))
+    )(back, msg, offsets, velocities, line(masses))
 
 
 def solution(mesh):

time: 94.4 us -> 92 us (0.975)
  blocking collectives: 27.7 us -> 44.2 us
  starting transfers between devices: 13.8 us -> 4.13 us
  waiting for transfers between devices: 7.36 us -> 0.01 us
  Pallas kernels: 43.7 us -> 42.6 us
    all_to_all x0 -> x1, blocking collectives: none -> 15.2 us  [per_device(): far = lax.all_to_all(ends, 'yhi', split_axis=0, concat_axis=0, tiled=True)]
    ppermute x1 -> x0, waiting for transfers between devices: 7.36 us -> none  [per_device(): far = lax.ppermute(ends, ('yhi', 'grp', 'mem'), swap)]
    all_to_all x1, starting transfers between devices: 9.8 us -> 4.13 us  [per_device(): msg = lax.all_to_all(msg, 'bead', split_axis=0, concat_axis=0, tiled=True)]
    ppermute x1 -> x0, starting transfers between devices: 4.04 us -> none  [per_device(): far = lax.ppermute(ends, ('yhi', 'grp', 'mem'), swap)]
    all_to_all x1, blocking collectives: 6.58 us -> 7.96 us  [per_device(): lax.all_to_all(done.reshape(GROUP, 2, 8, BLOCK), 'mem', split_axis=0, con...]
    pallas_call x2 -> x3, Pallas kernels: 2.87 us -> 2.29 us  [the longest x1 1.61 us: per_device(): pl.pallas_call(edges_kernel, out_shape=jax.ShapeDtypeStruct((8, 8, 256),...]
  transfers between devices with their start and end apart: 2 -> 1, of which waited for: 1 -> 0; matrix products, arithmetic and copies ran while one was open for 0% -> 0% of each run, Pallas kernels for 42% -> 42%
where the time goes in v3:
time: 92 us; the launch traced here: 91.6 us
  blocking collectives  44.2 us (48%)
  Pallas kernels  42.6 us (46%)
  starting transfers between devices  4.13 us (4%)
    pallas_call x1, Pallas kernels, call_main(): pl.pallas_call(main_kernel, out_shape=jax.ShapeDtypeStruct((2 * GROUP, 8,...  38.7 us
    all_to_all x1, blocking collectives, per_device(): lax.all_to_all(packed, ('grp', 'mem'), split_axis=0, concat_axis=0, tiled...  21 us
    all_to_all x1, blocking collectives, per_device(): far = lax.all_to_all(ends, 'yhi', split_axis=0, concat_axis=0, tiled=True)  15.2 us
    all_to_all x1, blocking collectives, per_device(): lax.all_to_all(done.reshape(GROUP, 2, 8, BLOCK), 'mem', split_axis=0, con...  7.96 us
    all_to_all x1, starting transfers between devices, per_device(): msg = lax.all_to_all(msg, 'bead', split_axis=0, concat_axis=0, tiled=True)  4.13 us
  transfers between devices with their start and end apart: 1, of which 0 were waited for; matrix products, arithmetic and copies ran while one was open for 0% of the time, Pallas kernels for 42%

profile of v3, /device:TPU:1, one launch (start us, length us, event | category | flops | bytes accessed | tf_op | source)
XLA Modules:
  0.0 91.6 jit_solution(17425546318550639337)
XLA Ops:
  0.6 1.6 %pack.1 = f32[16,8,256]{2,1,0:T(8,128)} custom-call(s32[2,4]{1,0:T(2,128)} %tiles_ref.1, f32[3,256]{1,0:T(4,128)} %cen_ref.1, f32[3,4,256]{2,1,0:T(4,128)} %off_ref.5, f32[3,4,256]{2,1,0:T(4,128)} %vel_ref.3, f32[1,256]{1,0:T(1,128)} %bitcast.8, f32[1,256]{1,0:T(1,128)} %bitcast.9, f32[1,256]{1,0:T(1,128)} %bitcast.6, s32[1,256]{1,0:T(1,128)} %bitcast.10), custom_call_target="tpu_custom_call" | custom-call | tf_op jit(solution)/shard_map/pack/pallas_call | solution.py:366
  2.2 21.0 %all_to_all.20.got_ref.v_ref = f32[16,8,256]{2,1,0:T(8,128)S(1)} all-to-all(f32[16,8,256]{2,1,0:T(8,128)} %pack.1), channel_id=1, replica_groups=mesh['yhi'=4,'grp'=4,'mem'=4,'bead'=8] {'grp','mem'}, dimensions={0} | all-to-all | bytes 262144 | tf_op jit(solution)/shard_map/all_to_all | solution.py:373
  23.2 15.2 %all_to_all.21.h_ref.far_ref = f32[4,5,8,256]{3,2,1,0:T(8,128)} all-to-all(f32[4,5,8,256]{3,2,1,0:T(8,128)S(1)} %middle.1), channel_id=1, replica_groups=mesh['yhi'=4,'grp'=4,'mem'=4,'bead'=8] {'yhi'}, dimensions={0} | all-to-all | bytes 327680 | tf_op jit(solution)/shard_map/all_to_all | solution.py:382
  38.5 0.0 copy-start
  38.5 1.6 %edges.1 = f32[8,8,256]{2,1,0:T(8,128)} custom-call(f32[4,5,8,256]{3,2,1,0:T(8,128)} %all_to_all.21.h_ref.far_ref, f32[3,4,256]{2,1,0:T(4,128)} %off_ref.5), custom_call_target="tpu_custom_call" | custom-call | tf_op jit(solution)/shard_map/edges/pallas_call | solution.py:383
  40.1 4.1 %all-to-all-start.2 = ((f32[8,8,256]{2,1,0:T(8,128)}), f32[8,8,256]{2,1,0:T(8,128)S(1)}, u32[]{:S(2)}, u32[]{:S(2)}) async-start(f32[8,8,256]{2,1,0:T(8,128)} %edges.1), calls=%async_computation.2 | async-start | bytes 131072 | tf_op jit(solution)/shard_map/all_to_all | solution.py:390
  44.2 0.0 copy-done
  44.2 38.7 %dipoles.1 = f32[8,8,128]{2,1,0:T(8,128)S(1)} custom-call(f32[16,8,256]{2,1,0:T(8,128)S(1)} %all_to_all.20.got_ref.v_ref, f32[4,5,8,256]{3,2,1,0:T(8,128)S(1)} %copy-done), custom_call_target="tpu_custom_call" | custom-call | flops 400000000 | bytes 300000 | tf_op jit(solution)/shard_map/dipoles/pallas_call | solution.py:338
  82.9 0.0 all-to-all-done.2.msg_ref
  82.9 0.0 copy-start.1
  82.9 0.0 copy-start.2
  83.0 0.0 copy-start.3
  83.0 8.0 %all_to_all.22.r_ref = f32[4,2,8,128]{3,2,1,0:T(8,128)S(1)} all-to-all(f32[4,2,8,128]{3,2,1,0:T(8,128)S(1)} %bitcast.5), channel_id=1, replica_groups=mesh['yhi'=4,'grp'=4,'mem'=4,'bead'=8] {'mem'}, dimensions={0} | all-to-all | bytes 65536 | tf_op jit(solution)/shard_map/all_to_all | solution.py:393
  90.9 0.0 copy-done.1
  90.9 0.0 copy-done.2
  90.9 0.0 copy-done.3
  90.9 0.6 finish.1
  (1 shorter events, 0.0 us)
Async XLA Ops:
  38.5 5.7 %copy-start = (f32[4,5,8,256]{3,2,1,0:T(8,128)S(1)}, f32[4,5,8,256]{3,2,1,0:T(8,128)}, u32[]{:S(2)}) copy-start(f32[4,5,8,256]{3,2,1,0:T(8,128)} %all_to_all.21.h_ref.far_ref) | copy-start | bytes 491524
  40.1 42.8 %all-to-all-start.2 = ((f32[8,8,256]{2,1,0:T(8,128)}), f32[8,8,256]{2,1,0:T(8,128)S(1)}, u32[]{:S(2)}, u32[]{:S(2)}) async-start(f32[8,8,256]{2,1,0:T(8,128)} %edges.1), calls=%async_computation.2 | async-start | bytes 131072 | tf_op jit(solution)/shard_map/all_to_all | solution.py:390
  82.9 8.0 %copy-start.1 = (f32[3,4,256]{2,1,0:T(4,128)S(1)}, f32[3,4,256]{2,1,0:T(4,128)}, u32[]{:S(2)}) copy-start(f32[3,4,256]{2,1,0:T(4,128)} %off_ref.5) | copy-start | bytes 36868
  82.9 8.0 %copy-start.2 = (f32[3,4,256]{2,1,0:T(4,128)S(1)}, f32[3,4,256]{2,1,0:T(4,128)}, u32[]{:S(2)}) copy-start(f32[3,4,256]{2,1,0:T(4,128)} %vel_ref.3) | copy-start | bytes 36868
  83.0 8.0 %copy-start.3 = (f32[256]{0:T(256)S(1)}, f32[256]{0:T(256)}, u32[]{:S(2)}) copy-start(f32[256]{0:T(256)} %param.13) | copy-start | bytes 3076

commit v4 on v3

--- a/solution.py
+++ b/solution.py
@@ -66,16 +66,28 @@
             out_ref[d * GROUP + r] = rows
 
 
+def fixed_point(x):
+    return jnp.clip(x * STEPS, -2147483648.0, 2147483520.0).astype(I32)
+
+
 def column(tile, c):
     return jnp.broadcast_to(tile[:, c : c + 1], (8, BLOCK))
 
 
-def rows_of(acc):
-    return jnp.broadcast_to(jnp.sum(jnp.transpose(acc), axis=0, keepdims=True), (8, BLOCK))
+def rows_of(acc, n):
+    if n not in (2,):
+        return jnp.broadcast_to(jnp.sum(jnp.transpose(acc), axis=0, keepdims=True), (8, BLOCK))
+    high = acc.astype(jnp.bfloat16)
+    rest = acc - high.astype(F32)
+    mid = rest.astype(jnp.bfloat16)
+    low = (rest - mid.astype(F32)).astype(jnp.bfloat16)
+    parts = jnp.concatenate([high, mid, low], axis=1)
+    ones = jnp.ones((8, 3 * BLOCK), jnp.bfloat16)
+    return lax.dot_general(ones, parts, (((1,), (1,)), ((), ())), preferred_element_type=F32)
 
 
 def main_kernel(
-    v_ref, h_ref, out_ref, srcf, srci, colf, coli, marks_v, marks, pair, acc, field, mu_a, mu_b, sem
+    v_ref, h_ref, out_ref, srcf, srci, colf, marks_v, marks, pair, acc, field, mu_a, mu_b, sem
 ):
     grp = lax.axis_index("grp")
     row = lax.axis_index("yhi")
@@ -84,17 +96,17 @@
     def load_slab(w, carry):
         r = grp * GROUP - HALO + w
         inside = jnp.logical_and(r >= 0, r < ROW)
-        near = lax.rem(jnp.where(r < 0, row + 3, row + 1), 4)
         far = jnp.where(r < 0, r + HALO, r - ROW)
         slab = row * ROW + r
         shift = jnp.where(slab < 0, -576.0, jnp.where(slab >= 64, 576.0, 0.0)).astype(F32)
-        whole = jnp.where(inside, v_ref[jnp.clip(r, 0, ROW - 1)], h_ref[near, jnp.clip(far, 0, HALO - 1)])
+        whole = jnp.where(inside, v_ref[jnp.clip(r, 0, ROW - 1)], h_ref[jnp.clip(far, 0, HALO - 1)])
         marks_v[pl.ds(w, 1), :] = whole[6:7, :BLOCK].astype(I32)
         for half in range(2):
             blk = 2 * w + half
             d = whole[:, half * BLOCK : (half + 1) * BLOCK]
             wrapped = d - box_side * jnp.floor(d * (1.0 / box_side) + 0.5)
-            fixed = jnp.clip(wrapped * STEPS, -2147483648.0, 2147483520.0).astype(I32)
+            fixed = fixed_point(wrapped)
+            d = jnp.where(jnp.logical_or(line == 1, line == 2), wrapped, d)
             d = jnp.where(line == 0, d + shift, d)
             d = jnp.where(line == 7, thole_coef**0.5 * lax.rsqrt(d[4:5]), d)
             for n, c in enumerate((0, 3, 7, 5, 4)):
@@ -104,10 +116,9 @@
                 srci[blk, n] = jnp.broadcast_to(fixed[n + 1 : n + 2], (8, BLOCK))
             at = pl.multiple_of(blk * BLOCK, BLOCK)
             colf[pl.ds(at, BLOCK), :] = jnp.transpose(jnp.where(line == 7, -d, d))
-            coli[pl.ds(at, BLOCK), :] = jnp.transpose(fixed)
         return carry
 
-    lax.fori_loop(0, WINDOW, load_slab, 0, unroll=7)
+    lax.fori_loop(0, WINDOW, load_slab, 0, unroll=14)
     copy = pltpu.make_async_copy(marks_v, marks, sem)
     copy.start()
     copy.wait()
@@ -118,29 +129,28 @@
 
     def targets(i, blk):
         at = pl.multiple_of(blk * BLOCK + i * 8, 8)
-        return colf[pl.ds(at, 8), :], coli[pl.ds(at, 8), :]
+        return colf[pl.ds(at, 8), :]
 
     def pipelined(start, stop, pairs, rows):
         def two(n, carry):
             blk = start + 2 * n
-            pairs(blk, 0)
-            rows(blk - 1, 1)
-            pairs(blk + 1, 1)
-            rows(blk, 0)
+            pairs(blk, 0, functools.partial(rows, blk - 1, 1))
+            pairs(blk + 1, 1, functools.partial(rows, blk, 0))
             return carry
 
         lax.fori_loop(0, (stop - start) // 2, two, 0)
-        rows(stop - 1, 1)
-
-    def field_block(blk, half):
+        for n in range(3):
+            rows(stop - 1, 1, n)
+
+    def field_block(blk, half, rows):
         src = [source(blk, k) for k in range(NT)]
         slot = jnp.where(jnp.logical_and(blk >= 4, blk < WBLK - 4), blk - 4, KEPT)
 
-        def tile(i, carry):
-            kf, ki = targets(i, blk)
+        def tile(i):
+            kf = targets(i, blk)
             xi, gi, idi = column(kf, 0), column(kf, 7), column(kf, 5)
-            yi, zi = column(ki, 1), column(ki, 2)
-            at = pl.multiple_of(i * 8, 8)
+            yi, zi = fixed_point(column(kf, 1)), fixed_point(column(kf, 2))
+            at = i * 8
             sums = [jnp.zeros((8, BLOCK), F32)] * 3
             for k in range(NT):
                 s = src[k]
@@ -165,24 +175,25 @@
                 sums = [sums[0] + w * dx, sums[1] + w * dy, sums[2] + w * dz]
             for n in range(3):
                 acc[half, n, pl.ds(at, 8), :] = sums[n]
-            return carry
-
-        lax.fori_loop(0, 16, tile, 0, unroll=16)
-
-    def field_rows(blk, half):
-        for n in range(3):
-            rows = rows_of(acc[half, n])
-            field[blk, n] = rows
-            mu_a[blk, n] = srcf[blk, 4] * rows
+
+        for i in range(16):
+            tile(i)
+            if i % 5 == 0 and i < 15:
+                rows(i // 5)
+
+    def field_rows(blk, half, n):
+        rows = rows_of(acc[half, n], n)
+        field[blk, n] = rows
+        mu_a[blk, n] = srcf[blk, 4] * rows
 
     pipelined(2, WBLK - 2, field_block, field_rows)
 
-    def mutual_block(old, blk, half):
+    def mutual_block(old, blk, half, rows):
         src = [source(blk, k) for k in range(NT)]
         mus = [[old[src[k], n] for n in range(3)] for k in range(NT)]
 
-        def tile(i, carry):
-            at = pl.multiple_of(i * 8, 8)
+        def tile(i):
+            at = i * 8
             sums = [jnp.zeros((8, BLOCK), F32)] * 3
             for k in range(NT):
                 dx, dy, dz, b3, b5 = [pair[blk - 4, k, n, pl.ds(at, 8), :] for n in range(5)]
@@ -195,13 +206,14 @@
                 ]
             for n in range(3):
                 acc[half, n, pl.ds(at, 8), :] = sums[n]
-            return carry
-
-        lax.fori_loop(0, 16, tile, 0, unroll=16)
-
-    def mutual_rows(new, blk, half):
-        for n in range(3):
-            new[blk, n] = srcf[blk, 4] * (field[blk, n] + rows_of(acc[half, n]))
+
+        for i in range(16):
+            tile(i)
+            if i % 5 == 0 and i < 15:
+                rows(i // 5)
+
+    def mutual_rows(new, blk, half, n):
+        new[blk, n] = srcf[blk, 4] * (field[blk, n] + rows_of(acc[half, n], n))
 
     old, new = mu_a, mu_b
     for step in range(ITERS):
@@ -233,11 +245,11 @@
         acc[0, 3, :, 0:8] = jnp.transpose(col)
 
         def tile(i, carry):
-            kf, ki = targets(i, blk)
+            kf = targets(i, blk)
             at = pl.multiple_of(i * 8, 8)
             km = acc[0, 3, pl.ds(at, 8), 0:8]
             xi, gi, idi, qi = column(kf, 0), column(kf, 7), column(kf, 5), column(kf, 3)
-            yi, zi = column(ki, 1), column(ki, 2)
+            yi, zi = fixed_point(column(kf, 1)), fixed_point(column(kf, 2))
             ax, ay, az = column(km, 0), column(km, 1), column(km, 2)
             fx, fy, fz, along = [jnp.zeros((8, BLOCK), F32)] * 4
             for c in range(6):
@@ -284,25 +296,25 @@
         res = jnp.zeros((8, BLOCK), F32)
         for n in range(3):
             res = jnp.where(line == n, own[n], res)
-            res = jnp.where(line == n + 3, rows_of(acc[0, n]), res)
+            res = jnp.where(line == n + 3, rows_of(acc[0, n], n), res)
         out_ref[n_own] = res
         return carry
 
     lax.fori_loop(0, 2 * GROUP, force_block, 0)
 
 
-def middle_kernel(got_ref, ends_ref):
-    row = lax.axis_index("yhi")
-    line = lax.broadcasted_iota(I32, (8, 256), 0)
-    kin = jnp.sum(got_ref[...], axis=0)
+def middle_kernel(got_ref, ends_ref, kin_ref):
+    start = jnp.where(lax.axis_index("grp") < 2, ROW - HALO, 0)
+    for n in range(HALO):
+        ends_ref[n] = got_ref[start + n]
+    kin = jnp.sum(got_ref[...], axis=0)[7:8, :BLOCK]
     for d in range(4):
-        start = jnp.where(lax.rem(row + 3, 4) == d, 0, ROW - HALO)
-        for n in range(HALO):
-            ends_ref[d, n] = jnp.where(line == 7, kin, got_ref[start + n])
-
-
-def edges_kernel(far_ref, off_ref, msg_ref):
-    kin = jnp.sum(far_ref[:, 0], axis=0)[7:8]
+        kin_ref[d] = kin
+
+
+def edges_kernel(kin_ref, off_ref, msg_ref):
+    kin = jnp.sum(kin_ref[...], axis=0)
+    kin = jnp.concatenate([kin, kin], axis=1)
     last = [off_ref[n, 3:4, :] for n in range(3)]
     first = [off_ref[n, 0:1, :] for n in range(3)]
     msg = jnp.concatenate(last + first + [kin, kin], axis=0)
@@ -344,7 +356,6 @@
             pltpu.VMEM((WBLK, 5, 8, BLOCK), F32),
             pltpu.VMEM((WBLK, 2, 8, BLOCK), I32),
             pltpu.VMEM((WBLK * BLOCK, 8), F32),
-            pltpu.VMEM((WBLK * BLOCK, 8), I32),
             pltpu.VMEM((16, BLOCK), I32),
             pltpu.SMEM((16, BLOCK), I32),
             pltpu.VMEM((KEPT + 1, NT, 5, BLOCK, BLOCK), F32),
@@ -371,22 +382,30 @@
         name="pack",
     )(tiles, centroids, offsets, velocities, line(charges), line(polar), line(masses), line(groups))
     got = lax.all_to_all(packed, ("grp", "mem"), split_axis=0, concat_axis=0, tiled=True)
-    ends = pl.pallas_call(
+    ends, kin = pl.pallas_call(
         middle_kernel,
-        out_shape=jax.ShapeDtypeStruct((4, HALO, 8, 256), F32),
+        out_shape=(jax.ShapeDtypeStruct((HALO, 8, 256), F32), jax.ShapeDtypeStruct((4, 1, BLOCK), F32)),
         in_specs=[VMEM],
-        out_specs=VMEM,
+        out_specs=(VMEM, VMEM),
         compiler_params=small,
         name="middle",
     )(got)
-    far = lax.all_to_all(ends, "yhi", split_axis=0, concat_axis=0, tiled=True)
+    swap = []
+    for y in range(4):
+        for i in range(ROW):
+            to = (y + (1 if i < ROW // 2 else -1)) % 4
+            swap.append((y * ROW + i, to * ROW + i))
+    far = lax.ppermute(ends, ("yhi", "grp", "mem"), swap)
+    kin = lax.all_to_all(kin, "yhi", split_axis=0, concat_axis=0, tiled=True)
+    kin, far = lax.optimization_barrier((kin, far))
     msg = pl.pallas_call(
         edges_kernel,
         out_shape=jax.ShapeDtypeStruct((8, 8, 256), F32),
         in_specs=[VMEM, VMEM],
         out_specs=VMEM,
+        compiler_params=small,
         name="edges",
-    )(far, offsets)
+    )(kin, offsets)
     msg = lax.all_to_all(msg, "bead", split_axis=0, concat_axis=0, tiled=True)
     done = call_main(got, far)
     done, msg = lax.optimization_barrier((done, msg))

time: 92 us -> 90.2 us (0.980)
  blocking collectives: 44.2 us -> 39.5 us
  starting transfers between devices: 4.13 us -> 8.35 us
  Pallas kernels: 42.6 us -> 41.2 us
    ppermute x0 -> x1, starting transfers between devices: none -> 4.22 us  [per_device(): far = lax.ppermute(ends, ('yhi', 'grp', 'mem'), swap)]
    all_to_all x1, blocking collectives: 15.2 us -> 11.3 us  [per_device(): kin = lax.all_to_all(kin, 'yhi', split_axis=0, concat_axis=0, tiled=True)]
    pallas_call x1, Pallas kernels: 1.61 us -> 0.64 us  [per_device(): pl.pallas_call(edges_kernel, out_shape=jax.ShapeDtypeStruct((8, 8, 256),...]
  transfers between devices with their start and end apart: 1 -> 2, of which waited for: 0 -> 0; matrix products, arithmetic and copies ran while one was open for 0% -> 0% of each run, Pallas kernels for 42% -> 43%
where the time goes in v4:
time: 90.2 us; the launch traced here: 89.7 us
  Pallas kernels  41.2 us (46%)
  blocking collectives  39.5 us (44%)
  starting transfers between devices  8.35 us (9%)
    pallas_call x1, Pallas kernels, call_main(): pl.pallas_call(main_kernel, out_shape=jax.ShapeDtypeStruct((2 * GROUP, 8,...  38.3 us
    all_to_all x1, blocking collectives, per_device(): lax.all_to_all(packed, ('grp', 'mem'), split_axis=0, concat_axis=0, tiled...  21 us
    all_to_all x1, blocking collectives, per_device(): kin = lax.all_to_all(kin, 'yhi', split_axis=0, concat_axis=0, tiled=True)  11.3 us
    all_to_all x1, blocking collectives, per_device(): lax.all_to_all(done.reshape(GROUP, 2, 8, BLOCK), 'mem', split_axis=0, con...  7.19 us
    ppermute x1, starting transfers between devices, per_device(): far = lax.ppermute(ends, ('yhi', 'grp', 'mem'), swap)  4.22 us
    all_to_all x1, starting transfers between devices, per_device(): msg = lax.all_to_all(msg, 'bead', split_axis=0, concat_axis=0, tiled=True)  4.13 us
  transfers between devices with their start and end apart: 2, of which 0 were waited for; matrix products, arithmetic and copies ran while one was open for 0% of the time, Pallas kernels for 43%

profile of v4, /device:TPU:1, one launch (start us, length us, event | category | flops | bytes accessed | tf_op | source)
XLA Modules:
  0.0 89.7 jit_solution(11778048041915367843)
XLA Ops:
  0.6 1.6 %pack.1 = f32[16,8,256]{2,1,0:T(8,128)} custom-call(s32[2,4]{1,0:T(2,128)} %tiles_ref.1, f32[3,256]{1,0:T(4,128)} %cen_ref.1, f32[3,4,256]{2,1,0:T(4,128)} %off_ref.5, f32[3,4,256]{2,1,0:T(4,128)} %vel_ref.3, f32[1,256]{1,0:T(1,128)} %bitcast.8, f32[1,256]{1,0:T(1,128)} %bitcast.9, f32[1,256]{1,0:T(1,128)} %bitcast.6, s32[1,256]{1,0:T(1,128)} %bitcast.10), custom_call_target="tpu_custom_call" | custom-call | tf_op jit(solution)/shard_map/pack/pallas_call | solution.py:377
  2.2 21.0 %all_to_all.20.got_ref.v_ref = f32[16,8,256]{2,1,0:T(8,128)S(1)} all-to-all(f32[16,8,256]{2,1,0:T(8,128)} %pack.1), channel_id=1, replica_groups=mesh['yhi'=4,'grp'=4,'mem'=4,'bead'=8] {'grp','mem'}, dimensions={0} | all-to-all | bytes 262144 | tf_op jit(solution)/shard_map/all_to_all | solution.py:384
  23.2 0.0 copy-start
  23.2 4.2 %collective-permute-start = (f32[5,8,256]{2,1,0:T(8,128)S(1)}, f32[5,8,256]{2,1,0:T(8,128)S(1)}, u32[]{:S(2)}, u32[]{:S(2)}) collective-permute-start(f32[5,8,256]{2,1,0:T(8,128)S(1)} %get-tuple-element.11), channel_id=1, source_target_pairs={{0,128},{8,136},{16,144},{24,152},{32,160},{40,168},{48,176},{56,1... | collective-permute-start | bytes 122888 | tf_op jit(solution)/shard_map/ppermute | solution.py:398
  27.5 11.3 %all_to_all.21.kin_ref = f32[4,1,128]{2,1,0:T(1,128)S(1)} all-to-all(f32[4,1,128]{2,1,0:T(1,128)S(1)} %get-tuple-element.10), channel_id=1, replica_groups=mesh['yhi'=4,'grp'=4,'mem'=4,'bead'=8] {'yhi'}, dimensions={0} | all-to-all | bytes 4096 | tf_op jit(solution)/shard_map/all_to_all | solution.py:399
  38.8 0.0 collective-permute-done.h_ref
  38.8 0.0 copy-done
  38.8 0.6 edges.1
  39.4 4.1 %all-to-all-start.2 = ((f32[8,8,256]{2,1,0:T(8,128)}), f32[8,8,256]{2,1,0:T(8,128)S(1)}, u32[]{:S(2)}, u32[]{:S(2)}) async-start(f32[8,8,256]{2,1,0:T(8,128)} %edges.1), calls=%async_computation.2 | async-start | bytes 131072 | tf_op jit(solution)/shard_map/all_to_all | solution.py:409
  43.6 38.3 %dipoles.1 = f32[8,8,128]{2,1,0:T(8,128)S(1)} custom-call(f32[16,8,256]{2,1,0:T(8,128)S(1)} %all_to_all.20.got_ref.v_ref, f32[5,8,256]{2,1,0:T(8,128)S(1)} %collective-permute-done.h_ref), custom_call_target="tpu_custom_call" | custom-call | flops 400000000 | bytes 300000 | tf_op jit(solution)/shard_map/dipoles/pallas_call | solution.py:350
  81.9 0.0 all-to-all-done.2.msg_ref
  81.9 0.0 copy-start.1
  81.9 0.0 copy-start.2
  81.9 7.2 %all_to_all.22.r_ref = f32[4,2,8,128]{3,2,1,0:T(8,128)S(1)} all-to-all(f32[4,2,8,128]{3,2,1,0:T(8,128)S(1)} %bitcast.5), channel_id=1, replica_groups=mesh['yhi'=4,'grp'=4,'mem'=4,'bead'=8] {'mem'}, dimensions={0} | all-to-all | bytes 65536 | tf_op jit(solution)/shard_map/all_to_all | solution.py:412
  89.1 0.0 copy-done.1
  89.1 0.0 copy-done.2
  89.1 0.7 finish.1
  (1 shorter events, 0.0 us)
Async XLA Ops:
  23.2 15.6 %copy-start = (f32[3,4,256]{2,1,0:T(4,128)S(1)}, f32[3,4,256]{2,1,0:T(4,128)}, u32[]{:S(2)}) copy-start(f32[3,4,256]{2,1,0:T(4,128)} %off_ref.5) | copy-start | bytes 36868
  23.2 15.6 %collective-permute-start = (f32[5,8,256]{2,1,0:T(8,128)S(1)}, f32[5,8,256]{2,1,0:T(8,128)S(1)}, u32[]{:S(2)}, u32[]{:S(2)}) collective-permute-start(f32[5,8,256]{2,1,0:T(8,128)S(1)} %get-tuple-element.11), channel_id=1, source_target_pairs={{0,128},{8,136},{16,144},{24,152},{32,160},{40,168},{48,176},{56,1... | collective-permute-start | bytes 122888 | tf_op jit(solution)/shard_map/ppermute | solution.py:398
  39.4 42.4 %all-to-all-start.2 = ((f32[8,8,256]{2,1,0:T(8,128)}), f32[8,8,256]{2,1,0:T(8,128)S(1)}, u32[]{:S(2)}, u32[]{:S(2)}) async-start(f32[8,8,256]{2,1,0:T(8,128)} %edges.1), calls=%async_computation.2 | async-start | bytes 131072 | tf_op jit(solution)/shard_map/all_to_all | solution.py:409
  81.9 7.2 %copy-start.1 = (f32[3,4,256]{2,1,0:T(4,128)S(1)}, f32[3,4,256]{2,1,0:T(4,128)}, u32[]{:S(2)}) copy-start(f32[3,4,256]{2,1,0:T(4,128)} %vel_ref.3) | copy-start | bytes 36868
  81.9 7.2 %copy-start.2 = (f32[256]{0:T(256)S(1)}, f32[256]{0:T(256)}, u32[]{:S(2)}) copy-start(f32[256]{0:T(256)} %param.13) | copy-start | bytes 3076

commit v5 on v4

--- a/solution.py
+++ b/solution.py
@@ -87,10 +87,10 @@
 
 
 def main_kernel(
-    v_ref, h_ref, out_ref, srcf, srci, colf, marks_v, marks, pair, acc, field, mu_a, mu_b, sem
+    place_ref, v_ref, h_ref, out_ref, srcf, srci, colf, marks_v, marks, pair, acc, field, mu_a, mu_b, fa, fb, sem
 ):
-    grp = lax.axis_index("grp")
-    row = lax.axis_index("yhi")
+    grp = place_ref[0]
+    row = place_ref[1]
     line = lax.broadcasted_iota(I32, (8, BLOCK), 0)
 
     def load_slab(w, carry):
@@ -222,88 +222,123 @@
         old, new = new, old
     mu = old
 
-    def force_block(n_own, carry):
+    def listed(t, src):
+        w = lax.div(t, 2)
+        count = jnp.float32(0.0)
+        for k in range(NT):
+            count = count + jnp.where(marks[w, lax.rem(t, 2) * NT + k] == src - 2 * (w - 1), 1.0, 0.0).astype(F32)
+        return count
+
+    def set_columns(blk, half):
+        own = [mu[blk, n] * (1.0 / UNIT) for n in range(3)]
+        acc[half, 3, :, 0:8] = jnp.transpose(jnp.where(line == 0, own[0], jnp.where(line == 1, own[1], own[2])))
+
+    def columns(i, blk, half):
+        kf = targets(i, blk)
+        km = acc[half, 3, i * 8 : i * 8 + 8, 0:8]
+        place = (column(kf, 0), fixed_point(column(kf, 1)), fixed_point(column(kf, 2)))
+        return place, column(kf, 7), column(kf, 5), column(kf, 3), [column(km, n) for n in range(3)]
+
+    def pair_force(cols, s, a, b):
+        (xi, yi, zi), gi, idi, qi, (ax, ay, az) = cols
+        half_sum = 0.5 * (a + b)
+        dx = xi - srcf[s, 0]
+        dy = (yi - srci[s, 0]).astype(F32) * (1.0 / STEPS)
+        dz = (zi - srci[s, 1]).astype(F32) * (1.0 / STEPS)
+        sq = dx * dx + dy * dy + dz * dz + 1.0
+        r = lax.rsqrt(sq)
+        gg = jnp.where(idi == srcf[s, 3], 0.0, gi * srcf[s, 2])
+        un = gg * sq * (sq * r)
+        f = jnp.exp(un)
+        l3 = 1.0 - f
+        unf = un * f
+        l5 = l3 + unf
+        t = jnp.maximum(cut_square - sq, 0.0)
+        r2 = r * r
+        p = t * (r2 * r)
+        pl3 = p * l3
+        b3 = t * pl3
+        pr = (3.0 * r2) * p
+        b5 = (t * pr) * l5
+        k3 = -4.0 * pl3 - b5
+        k5 = pr * (t * r2 * (1.5 * (un * unf) - 2.5 * l5) - 2.0 * l5)
+        bx, by, bz = mu[s, 0], mu[s, 1], mu[s, 2]
+        di = dx * ax + dy * ay + dz * az
+        dj = dx * bx + dy * by + dz * bz
+        mm = ax * bx + ay * by + az * bz
+        qa = a * srcf[s, 1]
+        qb = b * qi
+        k2 = k3 * (qa * di - qb * dj - half_sum * mm) + (2.0 * half_sum) * (k5 * (di * dj))
+        h = half_sum * b5
+        return qa * b3 + h * dj, h * di - qb * b3, (k2 * dx, k2 * dy, k2 * dz), (bx, by, bz)
+
+    zero = jnp.zeros((8, BLOCK), F32)
+
+    def across(step, carry):
+        w = step + HALO - 1
+        there = [[zero] * 4, [zero] * 4]
+        for half in range(2):
+            blk = 2 * w + half
+            set_columns(blk, half)
+            flags = [(listed(blk, 2 * w + 2 + e), listed(2 * w + 2 + e, blk)) for e in range(2)]
+            for i in range(16):
+                cols = columns(i, blk, half)
+                here = [zero] * 4
+                for e in range(2):
+                    coef, g, kd, bj = pair_force(cols, 2 * w + 2 + e, *flags[e])
+                    here = [here[n] + (g * bj[n] + kd[n]) for n in range(3)] + [here[3] + coef]
+                    there[e] = [there[e][n] + (coef * cols[4][n] + kd[n]) for n in range(3)] + [there[e][3] + g]
+                for n in range(3):
+                    fa[blk - 8, n, i * 8 : i * 8 + 8, :] = here[n] + here[3] * cols[4][n]
+        for e in range(2):
+            for n in range(3):
+                fb[2 * w + 2 + e - 8, n] = there[e][n] + there[e][3] * mu[2 * w + 2 + e, n]
+        return carry
+
+    lax.fori_loop(0, GROUP + 1, across, 0)
+
+    def within(step, carry):
+        first = 2 * (HALO + step)
+        second = first + 1
+        there = [zero] * 4
+        for half in range(2):
+            blk = first + half
+            set_columns(blk, half)
+            own = listed(blk, blk)
+            if half == 0:
+                pair_flags = (listed(first, second), listed(second, first))
+            for i in range(16):
+                cols = columns(i, blk, half)
+                coef, g, kd, bj = pair_force(cols, blk, own, own)
+                here = [g * bj[n] + kd[n] for n in range(3)] + [coef]
+                if half == 0:
+                    coef, g, kd, bj = pair_force(cols, second, *pair_flags)
+                    here = [here[n] + (g * bj[n] + kd[n]) for n in range(3)] + [here[3] + coef]
+                    there = [there[n] + (coef * cols[4][n] + kd[n]) for n in range(3)] + [there[3] + g]
+                for n in range(3):
+                    fa[blk - 8, n, i * 8 : i * 8 + 8, :] += here[n] + here[3] * cols[4][n]
+        for n in range(3):
+            fb[second - 8, n] += there[n] + there[3] * mu[second, n]
+        return carry
+
+    lax.fori_loop(0, GROUP, within, 0)
+
+    def finish_block(n_own, carry):
         blk = 2 * HALO + n_own
-        w = lax.div(blk, 2)
-        first = 2 * (w - 1)
-        a_of, b_of, c_of = [], [], []
-        for c in range(6):
-            s = first + c
-            ws = lax.div(s, 2)
-            here = jnp.float32(0.0)
-            there = jnp.float32(0.0)
-            for k in range(NT):
-                here = here + jnp.where(marks[w, lax.rem(blk, 2) * NT + k] == c, 1.0, 0.0).astype(F32)
-                there = there + jnp.where(
-                    marks[ws, lax.rem(s, 2) * NT + k] == blk - 2 * (ws - 1), 1.0, 0.0
-                ).astype(F32)
-            a_of.append(here)
-            b_of.append(there)
-            c_of.append(0.5 * (here + there))
-        own = [mu[blk, n] * (1.0 / UNIT) for n in range(3)]
-        col = jnp.where(line == 0, own[0], jnp.where(line == 1, own[1], own[2]))
-        acc[0, 3, :, 0:8] = jnp.transpose(col)
-
-        def tile(i, carry):
-            kf = targets(i, blk)
-            at = pl.multiple_of(i * 8, 8)
-            km = acc[0, 3, pl.ds(at, 8), 0:8]
-            xi, gi, idi, qi = column(kf, 0), column(kf, 7), column(kf, 5), column(kf, 3)
-            yi, zi = fixed_point(column(kf, 1)), fixed_point(column(kf, 2))
-            ax, ay, az = column(km, 0), column(km, 1), column(km, 2)
-            fx, fy, fz, along = [jnp.zeros((8, BLOCK), F32)] * 4
-            for c in range(6):
-                s = first + c
-                dx = xi - srcf[s, 0]
-                dy = (yi - srci[s, 0]).astype(F32) * (1.0 / STEPS)
-                dz = (zi - srci[s, 1]).astype(F32) * (1.0 / STEPS)
-                sq = dx * dx + dy * dy + dz * dz + 1.0
-                r = lax.rsqrt(sq)
-                gg = jnp.where(idi == srcf[s, 3], 0.0, gi * srcf[s, 2])
-                un = gg * sq * (sq * r)
-                f = jnp.exp(un)
-                l3 = 1.0 - f
-                unf = un * f
-                l5 = l3 + unf
-                t = jnp.maximum(cut_square - sq, 0.0)
-                r2 = r * r
-                p = t * (r2 * r)
-                pl3 = p * l3
-                b3 = t * pl3
-                pr = (3.0 * r2) * p
-                b5 = (t * pr) * l5
-                k3 = -4.0 * pl3 - b5
-                k5 = pr * (t * r2 * (1.5 * (un * unf) - 2.5 * l5) - 2.0 * l5)
-                bx, by, bz = mu[s, 0], mu[s, 1], mu[s, 2]
-                di = dx * ax + dy * ay + dz * az
-                dj = dx * bx + dy * by + dz * bz
-                mm = ax * bx + ay * by + az * bz
-                qa = a_of[c] * srcf[s, 1]
-                qb = b_of[c] * qi
-                k2 = k3 * (qa * di - qb * dj - c_of[c] * mm) + (2.0 * c_of[c]) * (k5 * (di * dj))
-                h = c_of[c] * b5
-                along = along + (qa * b3 + h * dj)
-                g = h * di - qb * b3
-                fx = fx + (g * bx + k2 * dx)
-                fy = fy + (g * by + k2 * dy)
-                fz = fz + (g * bz + k2 * dz)
-            acc[0, 0, pl.ds(at, 8), :] = fx + along * ax
-            acc[0, 1, pl.ds(at, 8), :] = fy + along * ay
-            acc[0, 2, pl.ds(at, 8), :] = fz + along * az
-            return carry
-
-        lax.fori_loop(0, 16, tile, 0, unroll=16)
-        res = jnp.zeros((8, BLOCK), F32)
+        res = zero
         for n in range(3):
-            res = jnp.where(line == n, own[n], res)
-            res = jnp.where(line == n + 3, rows_of(acc[0, n], n), res)
+            res = jnp.where(line == n, mu[blk, n] * (1.0 / UNIT), res)
+            back = jnp.sum(fb[blk - 8, n], axis=0, keepdims=True)
+            res = jnp.where(line == n + 3, rows_of(fa[blk - 8, n], n) - back, res)
         out_ref[n_own] = res
         return carry
 
-    lax.fori_loop(0, 2 * GROUP, force_block, 0)
-
-
-def middle_kernel(got_ref, ends_ref, kin_ref):
+    lax.fori_loop(0, 2 * GROUP, finish_block, 0, unroll=4)
+
+
+def middle_kernel(got_ref, ends_ref, kin_ref, place_ref):
+    place_ref[0] = lax.axis_index("grp")
+    place_ref[1] = lax.axis_index("yhi")
     start = jnp.where(lax.axis_index("grp") < 2, ROW - HALO, 0)
     for n in range(HALO):
         ends_ref[n] = got_ref[start + n]
@@ -346,11 +381,11 @@
         no_ref[n] = off + time_step * nv
 
 
-def call_main(got, far):
+def call_main(place, got, far):
     return pl.pallas_call(
         main_kernel,
         out_shape=jax.ShapeDtypeStruct((2 * GROUP, 8, BLOCK), F32),
-        in_specs=[VMEM, VMEM],
+        in_specs=[SMEM, VMEM, VMEM],
         out_specs=VMEM,
         scratch_shapes=[
             pltpu.VMEM((WBLK, 5, 8, BLOCK), F32),
@@ -363,12 +398,14 @@
             pltpu.VMEM((WBLK, 3, 8, BLOCK), F32),
             pltpu.VMEM((WBLK, 3, 8, BLOCK), F32),
             pltpu.VMEM((WBLK, 3, 8, BLOCK), F32),
+            pltpu.VMEM((10, 3, BLOCK, BLOCK), F32),
+            pltpu.VMEM((12, 3, 8, BLOCK), F32),
             pltpu.SemaphoreType.DMA,
         ],
         compiler_params=pltpu.CompilerParams(vmem_limit_bytes=50 * 2**20),
         cost_estimate=pl.CostEstimate(flops=400_000_000, bytes_accessed=300_000, transcendentals=0),
         name="dipoles",
-    )(got, far)
+    )(place, got, far)
 
 
 def per_device(centroids, offsets, velocities, charges, polar, masses, groups, tiles):
@@ -382,11 +419,11 @@
         name="pack",
     )(tiles, centroids, offsets, velocities, line(charges), line(polar), line(masses), line(groups))
     got = lax.all_to_all(packed, ("grp", "mem"), split_axis=0, concat_axis=0, tiled=True)
-    ends, kin = pl.pallas_call(
+    ends, kin, place = pl.pallas_call(
         middle_kernel,
-        out_shape=(jax.ShapeDtypeStruct((HALO, 8, 256), F32), jax.ShapeDtypeStruct((4, 1, BLOCK), F32)),
+        out_shape=(jax.ShapeDtypeStruct((HALO, 8, 256), F32), jax.ShapeDtypeStruct((4, 1, BLOCK), F32), jax.ShapeDtypeStruct((2,), I32)),
         in_specs=[VMEM],
-        out_specs=(VMEM, VMEM),
+        out_specs=(VMEM, VMEM, SMEM),
         compiler_params=small,
         name="middle",
     )(got)
@@ -407,7 +444,7 @@
         name="edges",
     )(kin, offsets)
     msg = lax.all_to_all(msg, "bead", split_axis=0, concat_axis=0, tiled=True)
-    done = call_main(got, far)
+    done = call_main(place, got, far)
     done, msg = lax.optimization_barrier((done, msg))
     back = lax.all_to_all(done.reshape(GROUP, 2, 8, BLOCK), "mem", split_axis=0, concat_axis=0, tiled=True)
     shape = jax.ShapeDtypeStruct((3, 4, 256), F32)

time: 90.2 us -> 87.5 us (0.970)
  Pallas kernels: 41.2 us -> 38.5 us
    pallas_call x1, Pallas kernels: 38.3 us -> 35 us  [call_main(): pl.pallas_call(main_kernel, out_shape=jax.ShapeDtypeStruct((2 * GROUP, 8,...]
  transfers between devices with their start and end apart: 2 -> 2, of which waited for: 0 -> 0; matrix products, arithmetic and copies ran while one was open for 0% -> 0% of each run, Pallas kernels for 43% -> 40%
where the time goes in v5:
time: 87.5 us; the launch traced here: 87 us
  blocking collectives  39.5 us (45%)
  Pallas kernels  38.5 us (44%)
  starting transfers between devices  8.35 us (10%)
    pallas_call x1, Pallas kernels, call_main(): pl.pallas_call(main_kernel, out_shape=jax.ShapeDtypeStruct((2 * GROUP, 8,...  35 us
    all_to_all x1, blocking collectives, per_device(): lax.all_to_all(packed, ('grp', 'mem'), split_axis=0, concat_axis=0, tiled...  21 us
    all_to_all x1, blocking collectives, per_device(): kin = lax.all_to_all(kin, 'yhi', split_axis=0, concat_axis=0, tiled=True)  11.3 us
    all_to_all x1, blocking collectives, per_device(): lax.all_to_all(done.reshape(GROUP, 2, 8, BLOCK), 'mem', split_axis=0, con...  7.19 us
    ppermute x1, starting transfers between devices, per_device(): far = lax.ppermute(ends, ('yhi', 'grp', 'mem'), swap)  4.22 us
    all_to_all x1, starting transfers between devices, per_device(): msg = lax.all_to_all(msg, 'bead', split_axis=0, concat_axis=0, tiled=True)  4.13 us
  transfers between devices with their start and end apart: 2, of which 0 were waited for; matrix products, arithmetic and copies ran while one was open for 0% of the time, Pallas kernels for 40%

profile of v5, /device:TPU:1, one launch (start us, length us, event | category | flops | bytes accessed | tf_op | source)
XLA Modules:
  0.0 87.0 jit_solution(16660944827604194194)
XLA Ops:
  0.6 1.6 %pack.1 = f32[16,8,256]{2,1,0:T(8,128)} custom-call(s32[2,4]{1,0:T(2,128)} %tiles_ref.1, f32[3,256]{1,0:T(4,128)} %cen_ref.1, f32[3,4,256]{2,1,0:T(4,128)} %off_ref.5, f32[3,4,256]{2,1,0:T(4,128)} %vel_ref.3, f32[1,256]{1,0:T(1,128)} %bitcast.8, f32[1,256]{1,0:T(1,128)} %bitcast.9, f32[1,256]{1,0:T(1,128)} %bitcast.6, s32[1,256]{1,0:T(1,128)} %bitcast.10), custom_call_target="tpu_custom_call" | custom-call | tf_op jit(solution)/shard_map/pack/pallas_call | solution.py:414
  2.2 21.0 %all_to_all.20.got_ref.v_ref = f32[16,8,256]{2,1,0:T(8,128)S(1)} all-to-all(f32[16,8,256]{2,1,0:T(8,128)} %pack.1), channel_id=1, replica_groups=mesh['yhi'=4,'grp'=4,'mem'=4,'bead'=8] {'grp','mem'}, dimensions={0} | all-to-all | bytes 262144 | tf_op jit(solution)/shard_map/all_to_all | solution.py:421
  23.2 0.0 copy-start
  23.2 0.6 middle.1
  23.8 4.2 %collective-permute-start = (f32[5,8,256]{2,1,0:T(8,128)S(1)}, f32[5,8,256]{2,1,0:T(8,128)S(1)}, u32[]{:S(2)}, u32[]{:S(2)}) collective-permute-start(f32[5,8,256]{2,1,0:T(8,128)S(1)} %get-tuple-element.13), channel_id=1, source_target_pairs={{0,128},{8,136},{16,144},{24,152},{32,160},{40,168},{48,176},{56,1... | collective-permute-start | bytes 122888 | tf_op jit(solution)/shard_map/ppermute | solution.py:435
  28.0 11.3 %all_to_all.21.kin_ref = f32[4,1,128]{2,1,0:T(1,128)S(1)} all-to-all(f32[4,1,128]{2,1,0:T(1,128)S(1)} %get-tuple-element.12), channel_id=1, replica_groups=mesh['yhi'=4,'grp'=4,'mem'=4,'bead'=8] {'yhi'}, dimensions={0} | all-to-all | bytes 4096 | tf_op jit(solution)/shard_map/all_to_all | solution.py:436
  39.4 0.0 collective-permute-done.h_ref
  39.4 0.0 copy-done
  39.4 0.6 edges.1
  40.0 4.1 %all-to-all-start.2 = ((f32[8,8,256]{2,1,0:T(8,128)}), f32[8,8,256]{2,1,0:T(8,128)S(1)}, u32[]{:S(2)}, u32[]{:S(2)}) async-start(f32[8,8,256]{2,1,0:T(8,128)} %edges.1), calls=%async_computation.2 | async-start | bytes 131072 | tf_op jit(solution)/shard_map/all_to_all | solution.py:446
  44.2 35.0 %dipoles.1 = f32[8,8,128]{2,1,0:T(8,128)S(1)} custom-call(s32[2]{0:T(128)S(1)} %get-tuple-element.11.place_ref, f32[16,8,256]{2,1,0:T(8,128)S(1)} %all_to_all.20.got_ref.v_ref, f32[5,8,256]{2,1,0:T(8,128)S(1)} %collective-permute-done.h_ref), custom_call_target="tpu_custom_call" | custom-call | flops 400000000 | bytes 300000 | tf_op jit(solution)/shard_map/dipoles/pallas_call | solution.py:385
  79.2 0.0 all-to-all-done.2.msg_ref
  79.2 0.0 copy-start.1
  79.2 0.0 copy-start.2
  79.2 7.2 %all_to_all.22.r_ref = f32[4,2,8,128]{3,2,1,0:T(8,128)S(1)} all-to-all(f32[4,2,8,128]{3,2,1,0:T(8,128)S(1)} %bitcast.5), channel_id=1, replica_groups=mesh['yhi'=4,'grp'=4,'mem'=4,'bead'=8] {'mem'}, dimensions={0} | all-to-all | bytes 65536 | tf_op jit(solution)/shard_map/all_to_all | solution.py:449
  86.4 0.0 copy-done.1
  86.4 0.0 copy-done.2
  86.4 0.6 finish.1
Async XLA Ops:
  23.2 16.2 %copy-start = (f32[3,4,256]{2,1,0:T(4,128)S(1)}, f32[3,4,256]{2,1,0:T(4,128)}, u32[]{:S(2)}) copy-start(f32[3,4,256]{2,1,0:T(4,128)} %off_ref.5) | copy-start | bytes 36868
  23.8 15.6 %collective-permute-start = (f32[5,8,256]{2,1,0:T(8,128)S(1)}, f32[5,8,256]{2,1,0:T(8,128)S(1)}, u32[]{:S(2)}, u32[]{:S(2)}) collective-permute-start(f32[5,8,256]{2,1,0:T(8,128)S(1)} %get-tuple-element.13), channel_id=1, source_target_pairs={{0,128},{8,136},{16,144},{24,152},{32,160},{40,168},{48,176},{56,1... | collective-permute-start | bytes 122888 | tf_op jit(solution)/shard_map/ppermute | solution.py:435
  40.0 39.1 %all-to-all-start.2 = ((f32[8,8,256]{2,1,0:T(8,128)}), f32[8,8,256]{2,1,0:T(8,128)S(1)}, u32[]{:S(2)}, u32[]{:S(2)}) async-start(f32[8,8,256]{2,1,0:T(8,128)} %edges.1), calls=%async_computation.2 | async-start | bytes 131072 | tf_op jit(solution)/shard_map/all_to_all | solution.py:446
  79.2 7.2 %copy-start.1 = (f32[3,4,256]{2,1,0:T(4,128)S(1)}, f32[3,4,256]{2,1,0:T(4,128)}, u32[]{:S(2)}) copy-start(f32[3,4,256]{2,1,0:T(4,128)} %vel_ref.3) | copy-start | bytes 36868
  79.2 7.2 %copy-start.2 = (f32[256]{0:T(256)S(1)}, f32[256]{0:T(256)}, u32[]{:S(2)}) copy-start(f32[256]{0:T(256)} %param.13) | copy-start | bytes 3076

commit v6 on v5

--- a/solution.py
+++ b/solution.py
@@ -182,7 +182,7 @@
                 rows(i // 5)
 
     def field_rows(blk, half, n):
-        rows = rows_of(acc[half, n], n)
+        rows = rows_of(acc[half, n], 0)
         field[blk, n] = rows
         mu_a[blk, n] = srcf[blk, 4] * rows
 

time: 87.5 us -> 86.8 us (level)
  no operation moved by 1% of the time
where the time goes in v6:
time: 86.8 us; the launch traced here: 86.3 us
  blocking collectives  39.5 us (46%)
  Pallas kernels  37.8 us (44%)
  starting transfers between devices  8.35 us (10%)
    pallas_call x1, Pallas kernels, call_main(): pl.pallas_call(main_kernel, out_shape=jax.ShapeDtypeStruct((2 * GROUP, 8,...  34.3 us
    all_to_all x1, blocking collectives, per_device(): lax.all_to_all(packed, ('grp', 'mem'), split_axis=0, concat_axis=0, tiled...  21 us
    all_to_all x1, blocking collectives, per_device(): kin = lax.all_to_all(kin, 'yhi', split_axis=0, concat_axis=0, tiled=True)  11.3 us
    all_to_all x1, blocking collectives, per_device(): lax.all_to_all(done.reshape(GROUP, 2, 8, BLOCK), 'mem', split_axis=0, con...  7.19 us
    ppermute x1, starting transfers between devices, per_device(): far = lax.ppermute(ends, ('yhi', 'grp', 'mem'), swap)  4.22 us
    all_to_all x1, starting transfers between devices, per_device(): msg = lax.all_to_all(msg, 'bead', split_axis=0, concat_axis=0, tiled=True)  4.13 us
  transfers between devices with their start and end apart: 2, of which 0 were waited for; matrix products, arithmetic and copies ran while one was open for 0% of the time, Pallas kernels for 40%

profile of v6, /device:TPU:1, one launch (start us, length us, event | category | flops | bytes accessed | tf_op | source)
XLA Modules:
  0.0 86.3 jit_solution(6542940190651681398)
XLA Ops:
  0.6 1.6 %pack.1 = f32[16,8,256]{2,1,0:T(8,128)} custom-call(s32[2,4]{1,0:T(2,128)} %tiles_ref.1, f32[3,256]{1,0:T(4,128)} %cen_ref.1, f32[3,4,256]{2,1,0:T(4,128)} %off_ref.5, f32[3,4,256]{2,1,0:T(4,128)} %vel_ref.3, f32[1,256]{1,0:T(1,128)} %bitcast.8, f32[1,256]{1,0:T(1,128)} %bitcast.9, f32[1,256]{1,0:T(1,128)} %bitcast.6, s32[1,256]{1,0:T(1,128)} %bitcast.10), custom_call_target="tpu_custom_call" | custom-call | tf_op jit(solution)/shard_map/pack/pallas_call | solution.py:414
  2.2 21.0 %all_to_all.20.got_ref.v_ref = f32[16,8,256]{2,1,0:T(8,128)S(1)} all-to-all(f32[16,8,256]{2,1,0:T(8,128)} %pack.1), channel_id=1, replica_groups=mesh['yhi'=4,'grp'=4,'mem'=4,'bead'=8] {'grp','mem'}, dimensions={0} | all-to-all | bytes 262144 | tf_op jit(solution)/shard_map/all_to_all | solution.py:421
  23.2 0.0 copy-start
  23.2 0.6 middle.1
  23.8 4.2 %collective-permute-start = (f32[5,8,256]{2,1,0:T(8,128)S(1)}, f32[5,8,256]{2,1,0:T(8,128)S(1)}, u32[]{:S(2)}, u32[]{:S(2)}) collective-permute-start(f32[5,8,256]{2,1,0:T(8,128)S(1)} %get-tuple-element.13), channel_id=1, source_target_pairs={{0,128},{8,136},{16,144},{24,152},{32,160},{40,168},{48,176},{56,1... | collective-permute-start | bytes 122888 | tf_op jit(solution)/shard_map/ppermute | solution.py:435
  28.0 11.3 %all_to_all.21.kin_ref = f32[4,1,128]{2,1,0:T(1,128)S(1)} all-to-all(f32[4,1,128]{2,1,0:T(1,128)S(1)} %get-tuple-element.12), channel_id=1, replica_groups=mesh['yhi'=4,'grp'=4,'mem'=4,'bead'=8] {'yhi'}, dimensions={0} | all-to-all | bytes 4096 | tf_op jit(solution)/shard_map/all_to_all | solution.py:436
  39.4 0.0 collective-permute-done.h_ref
  39.4 0.0 copy-done
  39.4 0.6 edges.1
  40.0 4.1 %all-to-all-start.2 = ((f32[8,8,256]{2,1,0:T(8,128)}), f32[8,8,256]{2,1,0:T(8,128)S(1)}, u32[]{:S(2)}, u32[]{:S(2)}) async-start(f32[8,8,256]{2,1,0:T(8,128)} %edges.1), calls=%async_computation.2 | async-start | bytes 131072 | tf_op jit(solution)/shard_map/all_to_all | solution.py:446
  44.2 34.3 %dipoles.1 = f32[8,8,128]{2,1,0:T(8,128)S(1)} custom-call(s32[2]{0:T(128)S(1)} %get-tuple-element.11.place_ref, f32[16,8,256]{2,1,0:T(8,128)S(1)} %all_to_all.20.got_ref.v_ref, f32[5,8,256]{2,1,0:T(8,128)S(1)} %collective-permute-done.h_ref), custom_call_target="tpu_custom_call" | custom-call | flops 400000000 | bytes 300000 | tf_op jit(solution)/shard_map/dipoles/pallas_call | solution.py:385
  78.5 0.0 all-to-all-done.2.msg_ref
  78.5 0.0 copy-start.1
  78.5 0.0 copy-start.2
  78.5 7.2 %all_to_all.22.r_ref = f32[4,2,8,128]{3,2,1,0:T(8,128)S(1)} all-to-all(f32[4,2,8,128]{3,2,1,0:T(8,128)S(1)} %bitcast.5), channel_id=1, replica_groups=mesh['yhi'=4,'grp'=4,'mem'=4,'bead'=8] {'mem'}, dimensions={0} | all-to-all | bytes 65536 | tf_op jit(solution)/shard_map/all_to_all | solution.py:449
  85.7 0.0 copy-done.1
  85.7 0.0 copy-done.2
  85.7 0.6 finish.1
Async XLA Ops:
  23.2 16.2 %copy-start = (f32[3,4,256]{2,1,0:T(4,128)S(1)}, f32[3,4,256]{2,1,0:T(4,128)}, u32[]{:S(2)}) copy-start(f32[3,4,256]{2,1,0:T(4,128)} %off_ref.5) | copy-start | bytes 36868
  23.8 15.6 %collective-permute-start = (f32[5,8,256]{2,1,0:T(8,128)S(1)}, f32[5,8,256]{2,1,0:T(8,128)S(1)}, u32[]{:S(2)}, u32[]{:S(2)}) collective-permute-start(f32[5,8,256]{2,1,0:T(8,128)S(1)} %get-tuple-element.13), channel_id=1, source_target_pairs={{0,128},{8,136},{16,144},{24,152},{32,160},{40,168},{48,176},{56,1... | collective-permute-start | bytes 122888 | tf_op jit(solution)/shard_map/ppermute | solution.py:435
  40.0 38.4 %all-to-all-start.2 = ((f32[8,8,256]{2,1,0:T(8,128)}), f32[8,8,256]{2,1,0:T(8,128)S(1)}, u32[]{:S(2)}, u32[]{:S(2)}) async-start(f32[8,8,256]{2,1,0:T(8,128)} %edges.1), calls=%async_computation.2 | async-start | bytes 131072 | tf_op jit(solution)/shard_map/all_to_all | solution.py:446
  78.5 7.2 %copy-start.1 = (f32[3,4,256]{2,1,0:T(4,128)S(1)}, f32[3,4,256]{2,1,0:T(4,128)}, u32[]{:S(2)}) copy-start(f32[3,4,256]{2,1,0:T(4,128)} %vel_ref.3) | copy-start | bytes 36868
  78.5 7.2 %copy-start.2 = (f32[256]{0:T(256)S(1)}, f32[256]{0:T(256)}, u32[]{:S(2)}) copy-start(f32[256]{0:T(256)} %param.13) | copy-start | bytes 3076
